TPU v7x, 512 devices: a whole 4x4x16 slice. The times are simulated.
512 devices in a mesh: dp: 32 (over y, x, core), tensor: 16 (over z).
Axes of the slice: x: 4, y: 4, z: 16, core: 2. Of those that a mesh axis runs over, the one named last changes fastest.
Arguments:
- ssm_state: float32 [64, 128, 64, 256], P('dp', 'tensor'), may hold values from -6 to 6
- conv_x: float32 [64, 3, 8192], P('dp', None, 'tensor'), may hold values from -6 to 6
- conv_bc: float32 [64, 3, 2048], P('dp'), may hold values from -6 to 6
- x_in: bfloat16 [3, 64, 8192], P(None, 'dp', 'tensor'), may hold values from -6 to 6
- bc_in: bfloat16 [3, 64, 2048], P(None, 'dp'), may hold values from -6 to 6
- z_in: bfloat16 [3, 64, 8192], P(None, 'dp', 'tensor'), may hold values from -6 to 6
- dt_in: bfloat16 [3, 64, 128], P(None, 'dp', 'tensor'), may hold values from -6 to 6
- conv_w_x: float32 [4, 8192], P(None, 'tensor'), may hold values from -3 to 3
- conv_w_bc: float32 [4, 2048], replicated, may hold values from -3 to 3
- dt_bias: float32 [128], P('tensor'), may hold values from -2 to 1
- a_rate: float32 [128], P('tensor'), may hold values from 0.05 to 4
- d_skip: float32 [128], P('tensor'), may hold values from 0.5 to 2
- norm_gain: float32 [8192], P('tensor'), may hold values from 0.1 to 1.9
- send_slot: int32 [3, 32], replicated, may hold values from 0 to 1
- dest_group: int32 [3, 32], replicated, may hold values from 0 to 31, each once within a row
- active: int32 [3, 64], P(None, 'dp'), may hold values 0 or 1
Outputs:
- mixer_out: bfloat16 [3, 64, 8192], P(None, 'dp', 'tensor')
- ssm_final: float32 [64, 128, 64, 256], P('dp', 'tensor')
- conv_x_final: float32 [64, 3, 8192], P('dp', None, 'tensor')
- conv_bc_final: float32 [64, 3, 2048], P('dp')
Inputs may be any that keep to these rules, and one draw needn't show every extreme that they name: dest_group[t] is a permutation of the 32 groups for every step t.
All inputs are finite; a program needn't handle non-finite values. No bound on the sum of `active` on one device may be relied on, other than what follows from the above.
Results may differ from a plain program's by a relative error of at most 0.002.
Values sent between devices are 32-bit elements; how exact they have to be, the bound alone decides.
A program may use at most 64 MiB of HBM per device.

v0:
```python
import jax
import jax.numpy as jnp
from jax import lax
from jax.sharding import PartitionSpec as P

HEADS = 128
GROUP_HEADS = 32
STEPS = 3


def group_onehot(heads_here):
    groups_count = HEADS // GROUP_HEADS
    group_here = lax.axis_index("tensor") * heads_here // GROUP_HEADS
    return (jnp.arange(groups_count, dtype=jnp.int32) == group_here).astype(jnp.float32)


def prepare(
    state,
    state_x,
    state_bc,
    x_new,
    bc_new,
    z_new,
    delta_raw,
    live_row,
    conv_w_x,
    conv_w_bc,
    dt_bias,
    a_rate,
    d_skip,
    norm_gain,
):
    rows, heads_here, width_p, width_n = state.shape
    groups_count = HEADS // GROUP_HEADS
    onehot = group_onehot(heads_here)
    window_x = jnp.concatenate([state_x, x_new.astype(jnp.float32)[:, None]], 1)
    window_bc = jnp.concatenate([state_bc, bc_new.astype(jnp.float32)[:, None]], 1)
    mixed_x = jax.nn.silu(jnp.sum(window_x * conv_w_x[None], 1)).reshape(rows, heads_here, width_p)
    mixed_bc = jax.nn.silu(jnp.sum(window_bc * conv_w_bc[None], 1)).reshape(
        rows, 2, groups_count, width_n
    )
    picked = jnp.sum(mixed_bc * onehot[None, None, :, None], axis=2)
    delta = jax.nn.softplus(delta_raw.astype(jnp.float32) + dt_bias[None])
    decay = jnp.exp(-delta * a_rate[None])
    fresh = (
        decay[:, :, None, None] * state
        + (delta[:, :, None] * mixed_x)[:, :, :, None] * picked[:, 0][:, None, None, :]
    )
    read = (
        jnp.einsum("rhpn,rn->rhp", fresh, picked[:, 1], precision=lax.Precision.HIGHEST)
        + d_skip[None, :, None] * mixed_x
    )
    gated = read.reshape(rows, heads_here * width_p) * jax.nn.silu(z_new.astype(jnp.float32))
    live = live_row > 0
    return (
        gated,
        jnp.where(live[:, None, None, None], fresh, state),
        jnp.where(live[:, None, None], window_x[:, 1:], state_x),
        jnp.where(live[:, None, None], window_bc[:, 1:], state_bc),
    )


def finish(gated, live_row, heads_here, width_p, norm_gain):
    onehot = group_onehot(heads_here)
    terms = jnp.sum(gated * gated, 1)[:, None] * onehot[None, :]
    totals = lax.psum(terms, "tensor")
    mean_square = jnp.sum(totals * onehot[None, :], 1) / (GROUP_HEADS * width_p)
    normed = gated * lax.rsqrt(mean_square + 1e-05)[:, None] * norm_gain[None]
    live = live_row > 0
    return jnp.where(live[:, None], normed, 0.0).astype(jnp.bfloat16)


def move_states(state, state_x, state_bc, slot, dest_row):
    rows, heads_here, width_p, width_n = state.shape
    ndevices = lax.axis_size("dp")
    flat_size = heads_here * width_p * width_n
    width_x = state_x.shape[2]
    width_bc = state_bc.shape[2]
    kernel_rows = state_x.shape[1]
    leaving_state = lax.dynamic_slice_in_dim(state, slot, 1, 0).reshape(
        1, 1, ndevices, flat_size // ndevices
    )
    leaving_x = lax.dynamic_slice_in_dim(state_x, slot, 1, 0).reshape(
        1, kernel_rows, ndevices, width_x // ndevices
    )
    leaving_bc = lax.dynamic_slice_in_dim(state_bc, slot, 1, 0).reshape(
        1, kernel_rows, ndevices, width_bc // ndevices
    )
    spread = (
        lax.all_to_all(leaving_state, "dp", split_axis=2, concat_axis=0, tiled=True),
        lax.all_to_all(leaving_x, "dp", split_axis=2, concat_axis=0, tiled=True),
        lax.all_to_all(leaving_bc, "dp", split_axis=2, concat_axis=0, tiled=True),
    )
    members = jnp.arange(ndevices, dtype=jnp.int32)
    anchor = jnp.sum(
        members[None, :] * (dest_row[None, :] == members[:, None]).astype(jnp.int32), axis=1
    )
    ordered = (
        jnp.take(spread[0], anchor, axis=0),
        jnp.take(spread[1], anchor, axis=0),
        jnp.take(spread[2], anchor, axis=0),
    )
    arrived = (
        lax.all_to_all(ordered[0], "dp", split_axis=0, concat_axis=2, tiled=True),
        lax.all_to_all(ordered[1], "dp", split_axis=0, concat_axis=2, tiled=True),
        lax.all_to_all(ordered[2], "dp", split_axis=0, concat_axis=2, tiled=True),
    )
    return (
        arrived[0].reshape(1, heads_here, width_p, width_n),
        arrived[1].reshape(1, kernel_rows, width_x),
        arrived[2].reshape(1, kernel_rows, width_bc),
    )


def local(
    ssm_state,
    conv_x,
    conv_bc,
    x_in,
    bc_in,
    z_in,
    dt_in,
    conv_w_x,
    conv_w_bc,
    dt_bias,
    a_rate,
    d_skip,
    norm_gain,
    send_slot,
    dest_group,
    active,
):
    group_index = lax.axis_index("dp")
    heads_here = ssm_state.shape[1]
    width_p = ssm_state.shape[2]
    weights = (conv_w_x, conv_w_bc, dt_bias, a_rate, d_skip, norm_gain)
    outputs = []
    for turn in range(STEPS):
        slot = send_slot[turn][group_index]
        arrived = move_states(ssm_state, conv_x, conv_bc, slot, dest_group[turn])
        ssm_state = lax.dynamic_update_slice_in_dim(ssm_state, arrived[0], slot, 0)
        conv_x = lax.dynamic_update_slice_in_dim(conv_x, arrived[1], slot, 0)
        conv_bc = lax.dynamic_update_slice_in_dim(conv_bc, arrived[2], slot, 0)
        gated, ssm_state, conv_x, conv_bc = prepare(
            ssm_state,
            conv_x,
            conv_bc,
            x_in[turn],
            bc_in[turn],
            z_in[turn],
            dt_in[turn],
            active[turn],
            *weights
        )
        outputs.append(finish(gated, active[turn], heads_here, width_p, norm_gain))
    return (jnp.stack(outputs, 0), ssm_state, conv_x, conv_bc)


def solution(mesh):
    return jax.shard_map(
        local,
        mesh=mesh,
        in_specs=(
            P("dp", "tensor", None, None),
            P("dp", None, "tensor"),
            P("dp", None, None),
            P(None, "dp", "tensor"),
            P(None, "dp", None),
            P(None, "dp", "tensor"),
            P(None, "dp", "tensor"),
            P(None, "tensor"),
            P(),
            P("tensor"),
            P("tensor"),
            P("tensor"),
            P("tensor"),
            P(),
            P(),
            P(None, "dp"),
        ),
        out_specs=(
            P(None, "dp", "tensor"),
            P("dp", "tensor", None, None),
            P("dp", None, "tensor"),
            P("dp", None, None),
        ),
        check_vma=False,
    )
```

profile of v0, /device:TPU:2, one launch (start us, length us, event | category | flops | bytes accessed | tf_op | source)
XLA Modules:
  0.0 305.5 jit_solution(6021489653969990280)
XLA Ops:
  7.4 9.6 %all-to-all-start.2 = ((f32[1,3,32,16]{3,0,1,2:T(1,128)}), f32[1,3,32,16]{3,0,1,2:T(1,128)S(1)}, u32[]{:S(2)}, u32[]{:S(2)}) async-start(f32[1,3,32,16]{3,0,1,2:T(1,128)} %copy.87), calls=%async_computation.2 | async-start | bytes 98304 | tf_op jit(solution)/shard_map/all_to_all | solution.py:91
  17.8 5.5 %all-to-all-done.2 = f32[1,3,32,16]{3,0,1,2:T(1,128)S(1)} async-done(((f32[1,3,32,16]{3,0,1,2:T(1,128)}), f32[1,3,32,16]{3,0,1,2:T(1,128)S(1)}, u32[]{:S(2)}, u32[]{:S(2)}) %all-to-all-start.2) | async-done | bytes 6176 | tf_op jit(solution)/shard_map/all_to_all | solution.py:91
  24.9 5.1 %all-to-all-start.3 = ((f32[32,3,1,16]{3,2,1,0:T(1,128)}), f32[32,3,1,16]{3,2,1,0:T(1,128)S(1)}, u32[]{:S(2)}, u32[]{:S(2)}) async-start(f32[32,3,1,16]{3,2,1,0:T(1,128)} %copy.90), calls=%async_computation.3 | async-start | bytes 98304 | tf_op jit(solution)/shard_map/all_to_all | solution.py:105
  42.3 6.3 %all-to-all-done.8 = f32[1,3,32,16]{3,0,1,2:T(1,128)S(1)} async-done(((f32[1,3,32,16]{3,0,1,2:T(1,128)}), f32[1,3,32,16]{3,0,1,2:T(1,128)S(1)}, u32[]{:S(2)}, u32[]{:S(2)}) %all-to-all-start.8) | async-done | bytes 6176 | tf_op jit(solution)/shard_map/all_to_all | solution.py:91
  75.8 5.0 %all-to-all-start.5 = ((f32[32,1,192]{2,1,0:T(1,128)}), f32[32,1,192]{2,1,0:T(1,128)S(1)}, u32[]{:S(2)}, u32[]{:S(2)}) async-start(f32[32,1,192]{2,1,0:T(1,128)} %reshape.829), calls=%async_computation.5 | async-start | bytes 65536 | tf_op jit(solution)/shard_map/all_to_all | solution.py:106
  81.6 5.4 %all-to-all-done.5 = f32[32,1,192]{2,1,0:T(1,128)S(1)} async-done(((f32[32,1,192]{2,1,0:T(1,128)}), f32[32,1,192]{2,1,0:T(1,128)S(1)}, u32[]{:S(2)}, u32[]{:S(2)}) %all-to-all-start.5) | async-done | bytes 24608 | tf_op jit(solution)/shard_map/all_to_all | solution.py:106
  87.1 5.0 %all-to-all-start.14 = ((f32[1,3,32,16]{3,0,1,2:T(1,128)}), f32[1,3,32,16]{3,0,1,2:T(1,128)S(1)}, u32[]{:S(2)}, u32[]{:S(2)}) async-start(f32[1,3,32,16]{3,0,1,2:T(1,128)} %copy.109), calls=%async_computation.14 | async-start | bytes 98304 | tf_op jit(solution)/shard_map/all_to_all | solution.py:91
  104.1 5.5 %all-to-all-done.10 = f32[32,1,192]{2,1,0:T(1,128)S(1)} async-done(((f32[32,1,192]{2,1,0:T(1,128)}), f32[32,1,192]{2,1,0:T(1,128)S(1)}, u32[]{:S(2)}, u32[]{:S(2)}) %all-to-all-start.10) | async-done | bytes 24608 | tf_op jit(solution)/shard_map/all_to_all | solution.py:92
  112.6 5.0 %all-to-all-start.11 = ((f32[32,1,192]{2,1,0:T(1,128)}), f32[32,1,192]{2,1,0:T(1,128)S(1)}, u32[]{:S(2)}, u32[]{:S(2)}) async-start(f32[32,1,192]{2,1,0:T(1,128)} %reshape.833), calls=%async_computation.11 | async-start | bytes 65536 | tf_op jit(solution)/shard_map/all_to_all | solution.py:106
  118.4 5.5 %all-to-all-done.11 = f32[32,1,192]{2,1,0:T(1,128)S(1)} async-done(((f32[32,1,192]{2,1,0:T(1,128)}), f32[32,1,192]{2,1,0:T(1,128)S(1)}, u32[]{:S(2)}, u32[]{:S(2)}) %all-to-all-start.11) | async-done | bytes 24608 | tf_op jit(solution)/shard_map/all_to_all | solution.py:106
  123.9 5.0 %all-to-all-start.15 = ((f32[32,3,1,16]{3,2,1,0:T(1,128)}), f32[32,3,1,16]{3,2,1,0:T(1,128)S(1)}, u32[]{:S(2)}, u32[]{:S(2)}) async-start(f32[32,3,1,16]{3,2,1,0:T(1,128)} %copy.112), calls=%async_computation.15 | async-start | bytes 98304 | tf_op jit(solution)/shard_map/all_to_all | solution.py:105
  146.5 5.1 %all-to-all-start = ((f32[1,1,32,4096]{3,1,0,2:T(1,128)}), f32[1,1,32,4096]{3,1,0,2:T(1,128)S(1)}, u32[]{:S(2)}, u32[]{:S(2)}) async-start(f32[1,1,32,4096]{3,1,0,2:T(1,128)} %reshape.623), calls=%async_computation | async-start | bytes 1048576 | tf_op jit(solution)/shard_map/all_to_all | solution.py:90
  155.5 6.7 %all-to-all-done = f32[1,1,32,4096]{3,1,0,2:T(1,128)S(1)} async-done(((f32[1,1,32,4096]{3,1,0,2:T(1,128)}), f32[1,1,32,4096]{3,1,0,2:T(1,128)S(1)}, u32[]{:S(2)}, u32[]{:S(2)}) %all-to-all-start) | async-done | bytes 524320 | tf_op jit(solution)/shard_map/all_to_all | solution.py:90
  162.2 5.0 %all-to-all-start.17 = ((f32[32,1,192]{2,1,0:T(1,128)}), f32[32,1,192]{2,1,0:T(1,128)S(1)}, u32[]{:S(2)}, u32[]{:S(2)}) async-start(f32[32,1,192]{2,1,0:T(1,128)} %reshape.837), calls=%async_computation.17 | async-start | bytes 65536 | tf_op jit(solution)/shard_map/all_to_all | solution.py:106
  173.6 5.0 %all-to-all-start.1 = ((f32[32,1,1,4096]{3,2,1,0:T(1,128)}), f32[32,1,1,4096]{3,2,1,0:T(1,128)S(1)}, u32[]{:S(2)}, u32[]{:S(2)}) async-start(f32[32,1,1,4096]{3,2,1,0:T(1,128)} %copy.86), calls=%async_computation.1 | async-start | bytes 1048576 | tf_op jit(solution)/shard_map/all_to_all | solution.py:104
  180.8 8.4 %all-to-all-done.1 = f32[32,1,1,4096]{3,2,1,0:T(1,128)S(1)} async-done(((f32[32,1,1,4096]{3,2,1,0:T(1,128)}), f32[32,1,1,4096]{3,2,1,0:T(1,128)S(1)}, u32[]{:S(2)}, u32[]{:S(2)}) %all-to-all-start.1) | async-done | bytes 524320 | tf_op jit(solution)/shard_map/all_to_all | solution.py:104
  192.1 15.2 %all_to_all.261 = f32[1,1,32,4096]{3,1,0,2:T(1,128)S(1)} all-to-all(f32[1,1,32,4096]{3,1,0,2:T(1,128)S(1)} %reshape.630), channel_id=1, replica_groups=mesh['dp'=32,'tensor'=16] {'dp'}, dimensions={2} | all-to-all | bytes 1048576 | tf_op jit(solution)/shard_map/all_to_all | solution.py:90
  209.8 5.0 %all-to-all-start.7 = ((f32[32,1,1,4096]{3,2,1,0:T(1,128)}), f32[32,1,1,4096]{3,2,1,0:T(1,128)S(1)}, u32[]{:S(2)}, u32[]{:S(2)}) async-start(f32[32,1,1,4096]{3,2,1,0:T(1,128)} %copy.97), calls=%async_computation.7 | async-start | bytes 1048576 | tf_op jit(solution)/shard_map/all_to_all | solution.py:104
  215.0 10.4 %all-to-all-done.7 = f32[32,1,1,4096]{3,2,1,0:T(1,128)S(1)} async-done(((f32[32,1,1,4096]{3,2,1,0:T(1,128)}), f32[32,1,1,4096]{3,2,1,0:T(1,128)S(1)}, u32[]{:S(2)}, u32[]{:S(2)}) %all-to-all-start.7) | async-done | bytes 524320 | tf_op jit(solution)/shard_map/all_to_all | solution.py:104
  228.5 5.2 %all-to-all-start.12 = ((f32[1,1,32,4096]{3,1,0,2:T(1,128)}), f32[1,1,32,4096]{3,1,0,2:T(1,128)S(1)}, u32[]{:S(2)}, u32[]{:S(2)}) async-start(f32[1,1,32,4096]{3,1,0,2:T(1,128)} %reshape.637), calls=%async_computation.12 | async-start | bytes 1048576 | tf_op jit(solution)/shard_map/all_to_all | solution.py:90
  234.8 9.5 %all-to-all-done.12 = f32[1,1,32,4096]{3,1,0,2:T(1,128)S(1)} async-done(((f32[1,1,32,4096]{3,1,0,2:T(1,128)}), f32[1,1,32,4096]{3,1,0,2:T(1,128)S(1)}, u32[]{:S(2)}, u32[]{:S(2)}) %all-to-all-start.12) | async-done | bytes 524320 | tf_op jit(solution)/shard_map/all_to_all | solution.py:90
  246.8 5.7 %all-to-all-start.13 = ((f32[32,1,1,4096]{3,2,1,0:T(1,128)}), f32[32,1,1,4096]{3,2,1,0:T(1,128)}, u32[]{:S(2)}, u32[]{:S(2)}) async-start(f32[32,1,1,4096]{3,2,1,0:T(1,128)} %copy.108), calls=%async_computation.13 | async-start | bytes 1048576 | tf_op jit(solution)/shard_map/all_to_all | solution.py:104
  256.2 6.9 %all-to-all-done.13 = f32[32,1,1,4096]{3,2,1,0:T(1,128)} async-done(((f32[32,1,1,4096]{3,2,1,0:T(1,128)}), f32[32,1,1,4096]{3,2,1,0:T(1,128)}, u32[]{:S(2)}, u32[]{:S(2)}) %all-to-all-start.13) | async-done | bytes 524320 | tf_op jit(solution)/shard_map/all_to_all | solution.py:104
  269.2 34.6 %all-reduce = (f32[2,4]{1,0:T(2,128)S(1)}, f32[2,4]{1,0:T(2,128)S(1)}, f32[2,4]{1,0:T(2,128)S(1)}) all-reduce(f32[2,4]{1,0:T(2,128)S(1)} %get-tuple-element.61, f32[2,4]{1,0:T(2,128)S(1)} %get-tuple-element.60, f32[2,4]{1,0:T(2,128)S(1)} %get-tuple-element.59), channel_id=1, replica_groups=mesh['dp'=32,'tensor'=16] {'tensor'}, use_global_device_ids=true, to_apply=%region_5.9 | all-reduce | flops 24 | bytes 192 | tf_op jit(solution)/shard_map/psum | solution.py:66
  (224 shorter events, 112.5 us)
Async XLA Ops:
  7.4 9.6 %copy-start.11 = (s32[3,32]{1,0:T(4,128)S(1)}, s32[3,32]{1,0:T(4,128)}, u32[]{:S(2)}) copy-start(s32[3,32]{1,0:T(4,128)} %param.36) | copy-start | bytes 1156
  7.4 15.9 %all-to-all-start.2 = ((f32[1,3,32,16]{3,0,1,2:T(1,128)}), f32[1,3,32,16]{3,0,1,2:T(1,128)S(1)}, u32[]{:S(2)}, u32[]{:S(2)}) async-start(f32[1,3,32,16]{3,0,1,2:T(1,128)} %copy.87), calls=%async_computation.2 | async-start | bytes 98304 | tf_op jit(solution)/shard_map/all_to_all | solution.py:91
  24.9 11.4 %all-to-all-start.3 = ((f32[32,3,1,16]{3,2,1,0:T(1,128)}), f32[32,3,1,16]{3,2,1,0:T(1,128)S(1)}, u32[]{:S(2)}, u32[]{:S(2)}) async-start(f32[32,3,1,16]{3,2,1,0:T(1,128)} %copy.90), calls=%async_computation.3 | async-start | bytes 98304 | tf_op jit(solution)/shard_map/all_to_all | solution.py:105
  37.3 11.3 %all-to-all-start.8 = ((f32[1,3,32,16]{3,0,1,2:T(1,128)}), f32[1,3,32,16]{3,0,1,2:T(1,128)S(1)}, u32[]{:S(2)}, u32[]{:S(2)}) async-start(f32[1,3,32,16]{3,0,1,2:T(1,128)} %copy.98), calls=%async_computation.8 | async-start | bytes 98304 | tf_op jit(solution)/shard_map/all_to_all | solution.py:91
  50.2 11.3 %all-to-all-start.9 = ((f32[32,3,1,16]{3,2,1,0:T(1,128)}), f32[32,3,1,16]{3,2,1,0:T(1,128)S(1)}, u32[]{:S(2)}, u32[]{:S(2)}) async-start(f32[32,3,1,16]{3,2,1,0:T(1,128)} %copy.101), calls=%async_computation.9 | async-start | bytes 98304 | tf_op jit(solution)/shard_map/all_to_all | solution.py:105
  57.4 9.1 %copy-start.3 = (bf16[3,2,2048]{2,1,0:T(2,128)(2,1)S(1)}, bf16[3,2,2048]{2,1,0:T(2,128)(2,1)}, u32[]{:S(2)}) copy-start(bf16[3,2,2048]{2,1,0:T(2,128)(2,1)} %param.26) | copy-start | bytes 73732
  61.5 11.3 %all-to-all-start.4 = ((f32[32,1,192]{2,1,0:T(1,128)}), f32[32,1,192]{2,1,0:T(1,128)S(1)}, u32[]{:S(2)}, u32[]{:S(2)}) async-start(f32[32,1,192]{2,1,0:T(1,128)} %reshape.827), calls=%async_computation.4 | async-start | bytes 65536 | tf_op jit(solution)/shard_map/all_to_all | solution.py:92
  75.8 11.3 %all-to-all-start.5 = ((f32[32,1,192]{2,1,0:T(1,128)}), f32[32,1,192]{2,1,0:T(1,128)S(1)}, u32[]{:S(2)}, u32[]{:S(2)}) async-start(f32[32,1,192]{2,1,0:T(1,128)} %reshape.829), calls=%async_computation.5 | async-start | bytes 65536 | tf_op jit(solution)/shard_map/all_to_all | solution.py:106
  87.1 11.3 %all-to-all-start.14 = ((f32[1,3,32,16]{3,0,1,2:T(1,128)}), f32[1,3,32,16]{3,0,1,2:T(1,128)S(1)}, u32[]{:S(2)}, u32[]{:S(2)}) async-start(f32[1,3,32,16]{3,0,1,2:T(1,128)} %copy.109), calls=%async_computation.14 | async-start | bytes 98304 | tf_op jit(solution)/shard_map/all_to_all | solution.py:91
  98.4 11.3 %all-to-all-start.10 = ((f32[32,1,192]{2,1,0:T(1,128)}), f32[32,1,192]{2,1,0:T(1,128)S(1)}, u32[]{:S(2)}, u32[]{:S(2)}) async-start(f32[32,1,192]{2,1,0:T(1,128)} %reshape.831), calls=%async_computation.10 | async-start | bytes 65536 | tf_op jit(solution)/shard_map/all_to_all | solution.py:92
  112.6 11.3 %all-to-all-start.11 = ((f32[32,1,192]{2,1,0:T(1,128)}), f32[32,1,192]{2,1,0:T(1,128)S(1)}, u32[]{:S(2)}, u32[]{:S(2)}) async-start(f32[32,1,192]{2,1,0:T(1,128)} %reshape.833), calls=%async_computation.11 | async-start | bytes 65536 | tf_op jit(solution)/shard_map/all_to_all | solution.py:106
  123.9 11.3 %all-to-all-start.15 = ((f32[32,3,1,16]{3,2,1,0:T(1,128)}), f32[32,3,1,16]{3,2,1,0:T(1,128)S(1)}, u32[]{:S(2)}, u32[]{:S(2)}) async-start(f32[32,3,1,16]{3,2,1,0:T(1,128)} %copy.112), calls=%async_computation.15 | async-start | bytes 98304 | tf_op jit(solution)/shard_map/all_to_all | solution.py:105
  135.2 11.3 %all-to-all-start.16 = ((f32[32,1,192]{2,1,0:T(1,128)}), f32[32,1,192]{2,1,0:T(1,128)S(1)}, u32[]{:S(2)}, u32[]{:S(2)}) async-start(f32[32,1,192]{2,1,0:T(1,128)} %reshape.835), calls=%async_computation.16 | async-start | bytes 65536 | tf_op jit(solution)/shard_map/all_to_all | solution.py:92
  146.5 5.2 %copy-start.13 = (f32[8]{0:T(128)S(1)}, f32[8]{0:T(128)}, u32[]{:S(2)}) copy-start(f32[8]{0:T(128)} %param.32) | copy-start | bytes 100
  146.5 5.2 %copy-start.14 = (f32[8]{0:T(128)S(1)}, f32[8]{0:T(128)}, u32[]{:S(2)}) copy-start(f32[8]{0:T(128)} %param.31) | copy-start | bytes 100
  146.5 15.7 %all-to-all-start = ((f32[1,1,32,4096]{3,1,0,2:T(1,128)}), f32[1,1,32,4096]{3,1,0,2:T(1,128)S(1)}, u32[]{:S(2)}, u32[]{:S(2)}) async-start(f32[1,1,32,4096]{3,1,0,2:T(1,128)} %reshape.623), calls=%async_computation | async-start | bytes 1048576 | tf_op jit(solution)/shard_map/all_to_all | solution.py:90
  162.2 11.3 %all-to-all-start.17 = ((f32[32,1,192]{2,1,0:T(1,128)}), f32[32,1,192]{2,1,0:T(1,128)S(1)}, u32[]{:S(2)}, u32[]{:S(2)}) async-start(f32[32,1,192]{2,1,0:T(1,128)} %reshape.837), calls=%async_computation.17 | async-start | bytes 65536 | tf_op jit(solution)/shard_map/all_to_all | solution.py:106
  169.7 8.8 %copy-start.6 = (f32[4,512]{1,0:T(4,128)S(1)}, f32[4,512]{1,0:T(4,128)}, u32[]{:S(2)}) copy-start(f32[4,512]{1,0:T(4,128)} %param.29) | copy-start | bytes 24580
  173.6 15.6 %all-to-all-start.1 = ((f32[32,1,1,4096]{3,2,1,0:T(1,128)}), f32[32,1,1,4096]{3,2,1,0:T(1,128)S(1)}, u32[]{:S(2)}, u32[]{:S(2)}) async-start(f32[32,1,1,4096]{3,2,1,0:T(1,128)} %copy.86), calls=%async_computation.1 | async-start | bytes 1048576 | tf_op jit(solution)/shard_map/all_to_all | solution.py:104
  209.8 15.7 %all-to-all-start.7 = ((f32[32,1,1,4096]{3,2,1,0:T(1,128)}), f32[32,1,1,4096]{3,2,1,0:T(1,128)S(1)}, u32[]{:S(2)}, u32[]{:S(2)}) async-start(f32[32,1,1,4096]{3,2,1,0:T(1,128)} %copy.97), calls=%async_computation.7 | async-start | bytes 1048576 | tf_op jit(solution)/shard_map/all_to_all | solution.py:104
  228.5 5.2 %copy-start.4 = (bf16[3,2,512]{2,1,0:T(2,128)(2,1)S(1)}, bf16[3,2,512]{2,1,0:T(2,128)(2,1)}, u32[]{:S(2)}) copy-start(bf16[3,2,512]{2,1,0:T(2,128)(2,1)} %param.27) | copy-start | bytes 18436
  228.5 15.8 %all-to-all-start.12 = ((f32[1,1,32,4096]{3,1,0,2:T(1,128)}), f32[1,1,32,4096]{3,1,0,2:T(1,128)S(1)}, u32[]{:S(2)}, u32[]{:S(2)}) async-start(f32[1,1,32,4096]{3,1,0,2:T(1,128)} %reshape.637), calls=%async_computation.12 | async-start | bytes 1048576 | tf_op jit(solution)/shard_map/all_to_all | solution.py:90
  245.4 7.8 %copy-start.1 = (f32[2,8,64,256]{3,2,1,0:T(8,128)S(1)}, f32[2,8,64,256]{3,2,1,0:T(8,128)}, u32[]{:S(2)}) copy-start(f32[2,8,64,256]{3,2,1,0:T(8,128)} %copy-done) | copy-start | bytes 3145732
  246.8 16.4 %all-to-all-start.13 = ((f32[32,1,1,4096]{3,2,1,0:T(1,128)}), f32[32,1,1,4096]{3,2,1,0:T(1,128)}, u32[]{:S(2)}, u32[]{:S(2)}) async-start(f32[32,1,1,4096]{3,2,1,0:T(1,128)} %copy.108), calls=%async_computation.13 | async-start | bytes 1048576 | tf_op jit(solution)/shard_map/all_to_all | solution.py:104
  (8 other events, 10.2 us)
where the time goes:
time: 307 us; the launch traced here: 306 us
  waiting for transfers between devices  97.7 us (32%)
  starting transfers between devices  90.2 us (29%)
  blocking collectives  49.8 us (16%)
  local copies, waits for them, and re-layouts  35.8 us (12%)
  other arithmetic  20.1 us (7%)
  between operations  7.39 us (2%)
  matrix products  4.47 us (1%)
    psum x1, blocking collectives, finish(): totals = lax.psum(terms, 'tensor')  34.6 us
    all_to_all x3, waiting for transfers between devices, move_states(): lax.all_to_all(ordered[0], 'dp', split_axis=0, concat_axis=2, tiled=True)  25.8 us
    all_to_all x3, starting transfers between devices, move_states(): lax.all_to_all(leaving_x, 'dp', split_axis=2, concat_axis=0, tiled=True)  19.4 us
    all_to_all x2, waiting for transfers between devices, move_states(): lax.all_to_all(leaving_state, 'dp', split_axis=2, concat_axis=0, tiled=True)  16.2 us
    all_to_all x3, starting transfers between devices, move_states(): lax.all_to_all(ordered[0], 'dp', split_axis=0, concat_axis=2, tiled=True)  15.7 us
    all_to_all x3, waiting for transfers between devices, move_states(): lax.all_to_all(leaving_x, 'dp', split_axis=2, concat_axis=0, tiled=True)  15.2 us
    all_to_all x1, blocking collectives, move_states(): lax.all_to_all(leaving_state, 'dp', split_axis=2, concat_axis=0, tiled=True)  15.2 us
    all_to_all x3, starting transfers between devices, move_states(): lax.all_to_all(ordered[1], 'dp', split_axis=0, concat_axis=2, tiled=True)  15 us
  transfers between devices with their start and end apart: 17, of which 17 were waited for; matrix products, arithmetic and copies ran while one was open for 8% of the time, Pallas kernels for 0%

commit v1 on v0

v1 whole, which is shorter than its diff:
```python
import jax
import jax.numpy as jnp
from jax import lax
from jax.experimental import pallas as pl
from jax.experimental.pallas import tpu as pltpu
from jax.sharding import PartitionSpec as P

MESH = pl.DeviceIdType.MESH
HIGH = lax.Precision.HIGHEST
STEPS = 3
SIDE = 4
CHIPS = 16
PLANE = 32
ROWS = 64
CHUNK = 32
HALF = 128
TENSOR = 16
GROUPS = 4
NORM_WIDTH = 2048

HOPS = (
    (2, 2), (2, 1), (1, 2), (2, 3), (3, 2), (2, 0), (0, 2), (1, 1),
    (3, 3), (1, 3), (3, 1), (1, 0), (0, 1), (3, 0), (0, 3), (0, 0),
)
OFFSETS = tuple(
    (kc, kx, ky) for kx, ky in HOPS for kc in (0, 1) if (kc, kx, ky) != (0, 0, 0)
)


def dot_nt(a, b, precision=HIGH):
    return lax.dot_general(
        a, b, (((1,), (1,)), ((), ())), precision=precision,
        preferred_element_type=jnp.float32,
    )


def dot_nn(a, b, precision=HIGH):
    return lax.dot_general(
        a, b, (((1,), (0,)), ((), ())), precision=precision,
        preferred_element_type=jnp.float32,
    )


def silu(v):
    return v / (1.0 + jnp.exp(-v))


def column(row_values, same):
    return jnp.sum(jnp.where(same, row_values, 0.0), axis=1, keepdims=True)


def kernel(
    ssm, bcp, xp, zp, dest, send, w16, wbc, dt_bias, a_rate, d_skip,
    out_s, out_g, out_tot, out_bc,
    pk, buf, sbuf, obuf, dxs, decs, mixed, hists, flat, ysend, yrecv,
    bcsend, bcrecv, sqsend, sqrecv, sidx_v, sidx_s,
    pk_ss, pk_rs, s_ss, s_rs, o_ss, o_rs, y_ss, y_rs, b_ss, b_rs, q_ss, q_rs, local_sem,
):
    d = lax.axis_index("dp")
    z = lax.axis_index("tensor")
    c = d % 2
    q = d // 2
    x = q % SIDE
    y = q // SIDE
    g = z // SIDE
    m = z % SIDE

    def at(offset):
        kc, kx, ky = offset
        cc = (c + kc) % 2
        qq = ((y + ky) % SIDE) * SIDE + (x + kx) % SIDE
        return qq * 2 + cc, qq, cc

    bc_peers = [
        (i, cc, (q * 2 + (c + cc) % 2, ((g + i) % GROUPS) * SIDE + m))
        for i in range(GROUPS)
        for cc in range(2)
        if (i, cc) != (0, 0)
    ]
    norm_peers = [(d, g * SIDE + (m + i) % SIDE) for i in range(1, SIDE)]

    barrier = pltpu.get_barrier_semaphore()
    signals = 0
    for offset in OFFSETS:
        pl.semaphore_signal(barrier, inc=1, device_id=(at(offset)[0], z), device_id_type=MESH)
        signals += 1
    for i, cc, peer in bc_peers:
        if i:
            pl.semaphore_signal(barrier, inc=1, device_id=peer, device_id_type=MESH)
            signals += 1
    for peer in norm_peers:
        pl.semaphore_signal(barrier, inc=1, device_id=peer, device_id_type=MESH)
        signals += 1

    def fill(qq, _):
        for cc in range(2):
            j = qq * 2 + cc
            for h in range(2):
                pk[j, h] = bcp[cc, h]
                pk[j, h, 6:7, :] = xp[qq, 0:1, HALF * h : HALF * (h + 1)]
                pk[j, h, 14:15, :] = xp[qq, 1:2, HALF * h : HALF * (h + 1)]
        return 0

    lax.fori_loop(0, CHIPS, fill, 0)
    pl.semaphore_wait(barrier, signals)

    def rows_of(device):
        return pl.ds(pl.multiple_of(device * 2, 2), 2)

    def small_copy(offset):
        p, _, _ = at(offset)
        return pltpu.make_async_remote_copy(
            src_ref=pk.at[p],
            dst_ref=buf.at[:, pl.ds(pl.multiple_of(d * 16, 16), 16)],
            send_sem=pk_ss.at[p], recv_sem=pk_rs.at[d],
            device_id=(p, z), device_id_type=MESH,
        )

    def small_arrival(p):
        return pltpu.make_async_remote_copy(
            src_ref=pk.at[p],
            dst_ref=buf.at[:, pl.ds(pl.multiple_of(p * 16, 16), 16)],
            send_sem=pk_ss.at[p], recv_sem=pk_rs.at[p],
            device_id=(p, z), device_id_type=MESH,
        )

    def slab(qq, cc):
        return (
            slice(None),
            pl.ds(pl.multiple_of(qq * CHUNK, CHUNK), CHUNK),
            pl.ds(pl.multiple_of(cc * HALF, HALF), HALF),
        )

    def state_copy(p, qq, cc, source):
        return pltpu.make_async_remote_copy(
            src_ref=ssm.at[slab(qq, cc)],
            dst_ref=sbuf.at[rows_of(source)],
            send_sem=s_ss.at[p], recv_sem=s_rs.at[source],
            device_id=(p, z), device_id_type=MESH,
        )

    own_small = pltpu.make_async_copy(
        pk.at[d], buf.at[:, pl.ds(pl.multiple_of(d * 16, 16), 16)], local_sem.at[0]
    )
    own_state = pltpu.make_async_copy(
        ssm.at[slab(q, c)], sbuf.at[rows_of(d)], local_sem.at[1]
    )
    for offset in OFFSETS:
        small_copy(offset).start()
    own_small.start()
    for offset in OFFSETS:
        p, qq, cc = at(offset)
        state_copy(p, qq, cc, d).start()
    own_state.start()

    down = lax.broadcasted_iota(jnp.int32, (ROWS, ROWS), 0)
    across = lax.broadcasted_iota(jnp.int32, (ROWS, ROWS), 1)
    same = down == across
    eye = same.astype(jnp.float32)
    moves = []
    picks = []
    for t in range(STEPS):
        dest_row = dest[t : t + 1, :]
        send_row = send[t : t + 1, :]
        send_col = jnp.sum(jnp.where(same, send_row, 0), axis=1, keepdims=True)
        arrives = (dest_row == down // 2) & (send_row == across % 2)
        moved = send_col == down % 2
        picks.append((moved & arrives) | (jnp.logical_not(moved) & same))
        moves.append(picks[t].astype(jnp.float32).astype(jnp.bfloat16))
    place2 = moves[2].astype(jnp.float32)
    place1 = dot_nn(moves[2], moves[1], None)
    place0 = dot_nn(place1.astype(jnp.bfloat16), moves[0], None)
    source = jnp.sum(jnp.where(picks[2], across, 0), axis=1, keepdims=True)
    for t in (1, 0):
        before = jnp.sum(jnp.where(picks[t], across, 0), axis=1, keepdims=True)
        before = jnp.sum(jnp.where(same, before, 0), axis=0, keepdims=True)
        source = jnp.sum(jnp.where(across == source, before, 0), axis=1, keepdims=True)
    source = jnp.sum(jnp.where(same, source, 0), axis=0, keepdims=True)
    source = jnp.minimum(jnp.maximum(source, 0), ROWS - 1)
    sidx_v[:, 0:ROWS] = jnp.broadcast_to(source, (8, ROWS))
    sidx_v[:, ROWS:] = jnp.zeros((8, ROWS), jnp.int32)
    to_scalar = pltpu.make_async_copy(sidx_v, sidx_s, local_sem.at[2])
    to_scalar.start()
    places = (place1, place2, eye)

    own_small.wait()
    for offset in OFFSETS:
        small_arrival(at(offset)[0]).wait_recv()

    def entry(e):
        return jnp.concatenate(
            [buf[h, pl.ds(e, ROWS, stride=8), :] for h in range(2)], axis=1
        )

    packed = entry(6)
    turned = jnp.transpose(packed)
    first = dot_nt(turned, place0)
    later = (dot_nt(turned, place1), dot_nt(turned, place2), turned)
    window = [first[CHUNK * k : CHUNK * (k + 1)] for k in range(3)]
    pick = (
        lax.broadcasted_iota(jnp.int32, (CHUNK, HALF), 0)
        == lax.broadcasted_iota(jnp.int32, (CHUNK, HALF), 1)
    ).astype(jnp.float32)
    weights = dot_nt(pick, w16[q])
    head = q // 2
    bias = dt_bias[head]
    rate = a_rate[head]
    skip = jnp.where(c == 0, d_skip[head], 0.0)
    live_cols = []
    skipped = []
    for t in range(STEPS):
        new = later[t][96 + CHUNK * t : 96 + CHUNK * (t + 1)]
        raw = later[t][192 + t : 193 + t] + bias
        live = later[t][195 + t : 196 + t]
        delta = jnp.maximum(raw, 0.0) + jnp.log1p(jnp.exp(-jnp.abs(raw)))
        decay = jnp.exp(-delta * rate)
        mixed_x = silu(
            window[0] * weights[:, 0:1]
            + window[1] * weights[:, 1:2]
            + window[2] * weights[:, 2:3]
            + new * weights[:, 3:4]
        )
        on = jnp.broadcast_to(live, (CHUNK, ROWS)) > 0.5
        dxs[t, :, 0:ROWS] = jnp.where(on, delta * mixed_x, 0.0)
        decs[t, :, 0:ROWS] = jnp.broadcast_to(
            jnp.where(live > 0.5, decay, 1.0), (8, ROWS)
        )
        skipped.append(skip * mixed_x)
        window = [
            jnp.where(on, window[1], window[0]),
            jnp.where(on, window[2], window[1]),
            jnp.where(on, new, window[2]),
        ]
        live_cols.append(column(live, same))

    window_bc = [dot_nn(place0, entry(e)) for e in range(3)]
    base = g * 2 * HALF + c * HALF
    w_b = wbc[:, pl.ds(pl.multiple_of(base, HALF), HALF)]
    w_c = wbc[:, pl.ds(pl.multiple_of(base + 1024, HALF), HALF)]
    w_bc = jnp.concatenate([w_b, w_c], axis=1)
    for t in range(STEPS):
        new = entry(3 + t)
        if t < 2:
            new = dot_nn(places[t], new)
        both = silu(
            window_bc[0] * w_bc[0:1]
            + window_bc[1] * w_bc[1:2]
            + window_bc[2] * w_bc[2:3]
            + new * w_bc[3:4]
        )
        mixed[t, 0] = both[:, :HALF]
        mixed[t, 1] = both[:, HALF:]
        on = jnp.broadcast_to(live_cols[t], (ROWS, 2 * HALF)) > 0.5
        window_bc = [
            jnp.where(on, window_bc[1], window_bc[0]),
            jnp.where(on, window_bc[2], window_bc[1]),
            jnp.where(on, new, window_bc[2]),
        ]
    for e in range(3):
        for h in range(2):
            hists[e, h] = window_bc[e][:, HALF * h : HALF * (h + 1)]

    def slot_row(e, h, cc, j):
        return hists[e, h, pl.ds(q * 4 + cc * 2 + j, 1), :]

    for shift in range(2):
        cc = (c + shift) % 2
        bcsend[shift] = jnp.zeros((8, 2 * HALF), jnp.float32)
        for e in range(3):
            for j in range(2):
                for h in range(2):
                    bcsend[
                        shift, e * 2 + j : e * 2 + j + 1, HALF * h : HALF * (h + 1)
                    ] = slot_row(e, h, cc, j)
    bc_copies = []
    for n, (i, shift, peer) in enumerate(bc_peers):
        copy = pltpu.make_async_remote_copy(
            src_ref=bcsend.at[shift], dst_ref=bcrecv.at[g * 2 + c],
            send_sem=b_ss.at[n], recv_sem=b_rs.at[n],
            device_id=peer, device_id_type=MESH,
        )
        copy.start()
        bc_copies.append(copy)
    own_bc = pltpu.make_async_copy(bcsend.at[0], bcrecv.at[g * 2 + c], local_sem.at[3])
    own_bc.start()

    to_scalar.wait()
    own_state.wait()
    for offset in OFFSETS:
        p, qq, cc = at(offset)
        state_copy(p, qq, cc, p).wait_recv()

    lane = lax.broadcasted_iota(jnp.int32, (CHUNK, HALF), 1)
    lane8 = lax.broadcasted_iota(jnp.int32, (8, HALF), 1)

    def advance(f, ys):
        state = sbuf[sidx_s[0, f]].reshape(4, 8, HALF)
        here = lane == f
        here8 = lane8 == f
        reads = []
        for t in range(STEPS):
            dx = jnp.sum(jnp.where(here, dxs[t], 0.0), axis=1, keepdims=True)
            dec = jnp.sum(jnp.where(here8, decs[t], 0.0), axis=1, keepdims=True)
            b_row = mixed[t, 0, pl.ds(f, 1), :]
            c_row = mixed[t, 1, pl.ds(f, 1), :]
            state = state * dec[None] + (dx * b_row).reshape(4, 8, HALF)
            read = jnp.sum(
                state.reshape(CHUNK, HALF) * c_row, axis=1, keepdims=True
            )
            reads.append(jnp.where(here, read, ys[t]))
        obuf[f] = state.reshape(CHUNK, HALF)
        return tuple(reads)

    def advance_some(i, ys):
        for k in range(4):
            ys = advance(i * 4 + k, ys)
        return ys

    zero = jnp.zeros((CHUNK, HALF), jnp.float32)
    ys = lax.fori_loop(0, ROWS // 4, advance_some, (zero,) * STEPS)

    pieces = [None] * 6
    for t in range(STEPS):
        read = ys[t][:, 0:ROWS] + skipped[t]
        back = eye if t == 2 else dot_nt(eye, places[t])
        pieces[t] = dot_nt(back, read)
        pieces[3 + t] = dot_nt(eye, window[t])
    for n in range(6):
        lo = CHUNK * (n % 4)
        flat[n // 4, :, lo : lo + CHUNK] = pieces[n]
    flat[1, :, 2 * CHUNK :] = jnp.zeros((ROWS, 2 * CHUNK), jnp.float32)

    def spread_rows(j, _):
        for n in range(2):
            for h in range(2):
                ysend[j, n : n + 1, HALF * h : HALF * (h + 1)] = flat[
                    h, pl.ds(j * 2 + n, 1), :
                ]
        return 0

    lax.fori_loop(0, PLANE, spread_rows, 0)

    def read_copy(p, source):
        return pltpu.make_async_remote_copy(
            src_ref=ysend.at[p], dst_ref=yrecv.at[source],
            send_sem=y_ss.at[p], recv_sem=y_rs.at[source],
            device_id=(p, z), device_id_type=MESH,
        )

    def final_copy(p, qq, cc, source):
        return pltpu.make_async_remote_copy(
            src_ref=obuf.at[rows_of(p)], dst_ref=out_s.at[slab(qq, cc)],
            send_sem=o_ss.at[p], recv_sem=o_rs.at[source],
            device_id=(p, z), device_id_type=MESH,
        )

    own_read = pltpu.make_async_copy(ysend.at[d], yrecv.at[d], local_sem.at[4])
    own_final = pltpu.make_async_copy(
        obuf.at[rows_of(d)], out_s.at[slab(q, c)], local_sem.at[5]
    )
    for offset in OFFSETS:
        read_copy(at(offset)[0], d).start()
    own_read.start()
    for offset in OFFSETS:
        final_copy(at(offset)[0], q, c, d).start()
    own_final.start()

    own_read.wait()
    for offset in OFFSETS:
        p = at(offset)[0]
        read_copy(p, p).wait_recv()
    lane2 = lax.broadcasted_iota(jnp.int32, (2, 2 * HALF), 1)
    total = jnp.zeros((2, 2 * HALF), jnp.float32)
    for qq in range(CHIPS):
        read = yrecv[2 * qq] + jnp.where(lane2 < 96, yrecv[2 * qq + 1], 0.0)
        gated = read * silu(zp[qq])
        out_g[qq] = jnp.where(lane2 < 96, gated, read)
        total = total + gated * gated
    fold = (
        lax.broadcasted_iota(jnp.int32, (2 * HALF, HALF), 0) // CHUNK
        == lax.broadcasted_iota(jnp.int32, (2 * HALF, HALF), 1)
    ).astype(jnp.float32)
    sqsend[...] = jnp.zeros((8, HALF), jnp.float32)
    sqsend[0:2, :] = dot_nn(total, fold)
    sq_copies = []
    for n, peer in enumerate(norm_peers):
        copy = pltpu.make_async_remote_copy(
            src_ref=sqsend, dst_ref=sqrecv.at[n],
            send_sem=q_ss.at[n], recv_sem=q_rs.at[n],
            device_id=peer, device_id_type=MESH,
        )
        copy.start()
        sq_copies.append(copy)
    for copy in bc_copies:
        copy.wait()
    own_bc.wait()
    out_bc[...] = bcrecv[...]
    for copy in sq_copies:
        copy.wait()
    out_tot[...] = sqsend[...] + sqrecv[0] + sqrecv[1] + sqrecv[2]

    own_final.wait()
    for offset in OFFSETS:
        p, qq, cc = at(offset)
        final_copy(p, qq, cc, p).wait_recv()
    for offset in OFFSETS:
        p, qq, cc = at(offset)
        small_copy(offset).wait_send()
        state_copy(p, qq, cc, d).wait_send()
        read_copy(p, d).wait_send()
        final_copy(p, q, c, d).wait_send()


def local(
    ssm_state, conv_x, conv_bc, x_in, bc_in, z_in, dt_in, conv_w_x, conv_w_bc,
    dt_bias, a_rate, d_skip, norm_gain, send_slot, dest_group, active,
):
    f32 = jnp.float32
    g = lax.axis_index("tensor") // SIDE

    bc_all = jnp.concatenate([conv_bc, jnp.swapaxes(bc_in, 0, 1).astype(f32)], axis=1)
    bc_all = lax.dynamic_index_in_dim(
        bc_all.reshape(2, 6, 2, GROUPS, 2, HALF), g, 3, keepdims=False
    )
    bcp = jnp.transpose(bc_all, (3, 2, 0, 1, 4))
    bcp = jnp.pad(bcp, ((0, 0),) * 3 + ((0, 2), (0, 0))).reshape(2, 2, 16, HALF)

    x_all = jnp.concatenate([conv_x, jnp.swapaxes(x_in, 0, 1).astype(f32)], axis=1)
    x_all = jnp.transpose(x_all.reshape(2, 6, CHIPS, CHUNK), (2, 0, 1, 3))
    dt_all = jnp.repeat(jnp.transpose(dt_in.astype(f32), (2, 1, 0)), 2, axis=0)
    live = jnp.broadcast_to(jnp.transpose(active).astype(f32)[None], (CHIPS, 2, STEPS))
    xp = jnp.concatenate(
        [x_all.reshape(CHIPS, 2, 192), dt_all, live, jnp.zeros((CHIPS, 2, 58), f32)],
        axis=2,
    )
    zp = jnp.transpose(z_in.astype(f32).reshape(STEPS, 2, CHIPS, CHUNK), (2, 1, 0, 3))
    zp = jnp.pad(zp.reshape(CHIPS, 2, 96), ((0, 0), (0, 0), (0, 160)))
    w16 = jnp.transpose(conv_w_x.reshape(4, CHIPS, CHUNK), (1, 0, 2))
    w16 = jnp.pad(w16, ((0, 0), (0, 4), (0, HALF - CHUNK)))
    dest2 = jnp.repeat(dest_group, 2, axis=1)
    send2 = jnp.repeat(send_slot, 2, axis=1)

    vmem = pl.BlockSpec(memory_space=pltpu.VMEM)
    smem = pl.BlockSpec(memory_space=pltpu.SMEM)
    hbm = pl.BlockSpec(memory_space=pl.ANY)
    dma = pltpu.SemaphoreType.DMA
    out_s, out_g, out_tot, out_bc = pl.pallas_call(
        kernel,
        out_shape=(
            jax.ShapeDtypeStruct((2, 512, 256), f32),
            jax.ShapeDtypeStruct((CHIPS, 2, 256), f32),
            jax.ShapeDtypeStruct((8, HALF), f32),
            jax.ShapeDtypeStruct((8, 8, 256), f32),
        ),
        in_specs=[hbm] + [vmem] * 7 + [smem] * 3,
        out_specs=(hbm, vmem, vmem, vmem),
        scratch_shapes=[
            pltpu.VMEM((PLANE, 2, 16, HALF), f32),
            pltpu.VMEM((2, PLANE * 16, HALF), f32),
            pltpu.VMEM((ROWS, CHUNK, HALF), f32),
            pltpu.VMEM((ROWS, CHUNK, HALF), f32),
            pltpu.VMEM((STEPS, CHUNK, HALF), f32),
            pltpu.VMEM((STEPS, 8, HALF), f32),
            pltpu.VMEM((STEPS, 2, ROWS, HALF), f32),
            pltpu.VMEM((3, 2, ROWS, HALF), f32),
            pltpu.VMEM((2, ROWS, HALF), f32),
            pltpu.VMEM((PLANE, 2, 256), f32),
            pltpu.VMEM((PLANE, 2, 256), f32),
            pltpu.VMEM((2, 8, 256), f32),
            pltpu.VMEM((8, 8, 256), f32),
            pltpu.VMEM((8, HALF), f32),
            pltpu.VMEM((3, 8, HALF), f32),
            pltpu.VMEM((8, HALF), jnp.int32),
            pltpu.SMEM((8, HALF), jnp.int32),
            dma((PLANE,)), dma((PLANE,)),
            dma((PLANE,)), dma((PLANE,)),
            dma((PLANE,)), dma((PLANE,)),
            dma((PLANE,)), dma((PLANE,)),
            dma((8,)), dma((8,)),
            dma((4,)), dma((4,)),
            dma((8,)),
        ],
        compiler_params=pltpu.CompilerParams(
            collective_id=0, has_side_effects=True, vmem_limit_bytes=48 * 2**20
        ),
    )(
        ssm_state.reshape(2, 512, 256), bcp, xp, zp, dest2, send2, w16, conv_w_bc,
        dt_bias, a_rate, d_skip,
    )

    factor = lax.rsqrt(out_tot[0:2, 0:STEPS] / NORM_WIDTH + 1e-05)
    packed = out_g[:, :, 0:192].reshape(CHIPS, 2, 6, CHUNK)
    normed = (
        packed[:, :, 0:3] * factor[None, :, :, None]
        * norm_gain.reshape(CHIPS, 1, 1, CHUNK)
    )
    normed = jnp.where(jnp.transpose(active)[None, :, :, None] > 0, normed, 0.0)
    mixer = jnp.transpose(normed.astype(jnp.bfloat16), (2, 1, 0, 3)).reshape(STEPS, 2, 512)
    final_x = jnp.transpose(packed[:, :, 3:6], (1, 2, 0, 3)).reshape(2, 3, 512)
    final_bc = out_bc[:, 0:6].reshape(GROUPS, 2, 3, 2, 2, HALF)
    final_bc = jnp.transpose(final_bc, (3, 2, 4, 0, 1, 5)).reshape(2, 3, 2048)
    return mixer, out_s.reshape(ssm_state.shape), final_x, final_bc


def solution(mesh):
    return jax.shard_map(
        local,
        mesh=mesh,
        in_specs=(
            P("dp", "tensor", None, None),
            P("dp", None, "tensor"),
            P("dp", None, None),
            P(None, "dp", "tensor"),
            P(None, "dp", None),
            P(None, "dp", "tensor"),
            P(None, "dp", "tensor"),
            P(None, "tensor"),
            P(),
            P("tensor"),
            P("tensor"),
            P("tensor"),
            P("tensor"),
            P(),
            P(),
            P(None, "dp"),
        ),
        out_specs=(
            P(None, "dp", "tensor"),
            P("dp", "tensor", None, None),
            P("dp", None, "tensor"),
            P("dp", None, None),
        ),
        check_vma=False,
    )
```

time: 307 us -> 69.1 us (0.23)
  the two profiles are of different devices: /device:TPU:2 before, /device:TPU:1 now
where the time goes in v1:
time: 69.1 us; the launch traced here: 68.8 us
  Pallas kernels  60.5 us (88%)
  local copies, waits for them, and re-layouts  7.03 us (10%)
  between operations  1.02 us (1%)
    pallas_call x1, Pallas kernels, local(): pl.pallas_call(kernel, out_shape=(jax.ShapeDtypeStruct((2, 512, 256), f32...  60.5 us
    unnamed x34, local copies, waits for them, and re-layouts  3.53 us

profile of v1, /device:TPU:1, one launch (start us, length us, event | category | flops | bytes accessed | tf_op | source)
XLA Modules:
  0.0 68.8 jit_solution(2759050807188047730)
XLA Ops:
  0.8 0.6 copy-done.15
  1.3 0.1 pad.21.clone
  1.4 0.1 copy.51
  1.5 0.1 mul.20
  1.7 0.1 reshape.73
  1.8 0.1 reshape.74
  1.9 0.1 reshape.77
  2.1 0.1 reshape.68
  2.3 0.7 copy-done.12
  3.0 0.1 broadcast_in_dim.37
  3.1 0.1 reshape.76.send
  3.2 0.6 copy-done.13
  3.8 0.1 reshape.75.dest
  3.9 0.1 reshape.70
  4.1 0.1 reshape.71
  4.3 0.1 maximum_maximum_fusion.xp
  4.4 0.6 copy-done.1
  5.0 60.5 %shard_map.183 = (f32[2,512,256]{2,1,0:T(8,128)S(1)}, f32[16,2,256]{2,1,0:T(2,128)S(1)}, f32[8,128]{1,0:T(8,128)S(1)}, f32[8,8,256]{2,1,0:T(8,128)S(1)}) custom-call(f32[2,512,256]{2,1,0:T(8,128)S(1)} %bitcast.55, f32[2,2,16,128]{3,2,1,0:T(8,128)S(1)} %pad_bitcast_fusion.bcp, f32[16,2,256]{2,1,0:T(2,128)S(1)} %maximum_maximum_fusion.xp, ...), custom_call_target="tpu_custom_call" | custom-call | tf_op jit(solution)/shard_map/pallas_call | solution.py:447
  65.6 0.7 reshape.83
  66.3 0.1 reshape.78
  66.4 0.1 slice_bitcast_fusion
  66.5 0.7 %reshape.81 = f32[2,3,512]{2,0,1:T(2,128)} reshape(f32[2,3,16,32]{3,2,0,1:T(8,128)S(1)} %copy.45) | data formatting | bytes 24576 | tf_op jit(solution)/shard_map/reshape | solution.py:499
  67.2 0.7 %reshape.79 = bf16[3,2,512]{2,1,0:T(2,128)(2,1)} reshape(bf16[3,2,16,32]{3,2,1,0:T(8,128)(2,1)S(1)} %copy.44) | data formatting | bytes 12288 | tf_op jit(solution)/shard_map/reshape | solution.py:498
  67.8 1.0 %copy.61 = f32[2,8,64,256]{3,2,1,0:T(8,128)} copy(f32[2,8,64,256]{3,2,1,0:T(8,128)S(1)} %bitcast.56) | data formatting | bytes 2097152
  (55 shorter events, 0.5 us)
Async XLA Ops:
  0.6 0.7 copy-start.15
  0.6 0.8 %copy-start.14 = (bf16[3,2,8]{2,1,0:T(2,128)(2,1)S(1)}, bf16[3,2,8]{2,1,0:T(2,128)(2,1)}, u32[]{:S(2)}) copy-start(bf16[3,2,8]{2,1,0:T(2,128)(2,1)} %param.22) | copy-start | bytes 292
  0.7 1.4 %copy-start.5 = (f32[2,3,2048]{2,0,1:T(2,128)S(1)}, f32[2,3,2048]{2,0,1:T(2,128)}, u32[]{:S(2)}) copy-start(f32[2,3,2048]{2,0,1:T(2,128)} %param.18) | copy-start | bytes 147460
  0.7 0.9 %copy-start.11 = (f32[512]{0:T(512)S(1)}, f32[512]{0:T(512)}, u32[]{:S(2)}) copy-start(f32[512]{0:T(512)} %param.28) | copy-start | bytes 6148
  0.7 0.9 %copy-start.9 = (bf16[3,2,512]{2,1,0:T(2,128)(2,1)S(1)}, bf16[3,2,512]{2,1,0:T(2,128)(2,1)}, u32[]{:S(2)}) copy-start(bf16[3,2,512]{2,1,0:T(2,128)(2,1)} %param.19) | copy-start | bytes 18436
  0.7 1.2 %copy-start.8 = (f32[4,512]{1,0:T(4,128)S(1)}, f32[4,512]{1,0:T(4,128)}, u32[]{:S(2)}) copy-start(f32[4,512]{1,0:T(4,128)} %param.23) | copy-start | bytes 24580
  0.7 0.9 %copy-start.7 = (f32[2,3,512]{2,0,1:T(2,128)S(1)}, f32[2,3,512]{2,0,1:T(2,128)}, u32[]{:S(2)}) copy-start(f32[2,3,512]{2,0,1:T(2,128)} %param.17) | copy-start | bytes 36868
  0.7 0.9 %copy-start.10 = (bf16[3,2,512]{2,1,0:T(2,128)(2,1)S(1)}, bf16[3,2,512]{2,1,0:T(2,128)(2,1)}, u32[]{:S(2)}) copy-start(bf16[3,2,512]{2,1,0:T(2,128)(2,1)} %param.21) | copy-start | bytes 18436
  0.7 1.3 %copy-start.6 = (bf16[3,2,2048]{2,1,0:T(2,128)(2,1)S(1)}, bf16[3,2,2048]{2,1,0:T(2,128)(2,1)}, u32[]{:S(2)}) copy-start(bf16[3,2,2048]{2,1,0:T(2,128)(2,1)} %param.20) | copy-start | bytes 73732
  0.7 3.7 %copy-start = (f32[2,8,64,256]{3,2,1,0:T(8,128)S(1)}, f32[2,8,64,256]{3,2,1,0:T(8,128)}, u32[]{:S(2)}) copy-start(f32[2,8,64,256]{3,2,1,0:T(8,128)} %param.16) | copy-start | bytes 3145732
  2.3 0.7 copy-start.12
  3.1 0.7 %copy-start.13 = (s32[3,32]{1,0:T(4,128)S(1)}, s32[3,32]{1,0:T(4,128)}, u32[]{:S(2)}) copy-start(s32[3,32]{1,0:T(4,128)} %param.30) | copy-start | bytes 1156
  4.3 0.8 %copy-start.1 = (f32[4,2048]{1,0:T(4,128)S(1)}, f32[4,2048]{1,0:T(4,128)}, u32[]{:S(2)}) copy-start(f32[4,2048]{1,0:T(4,128)} %wbc.1) | copy-start | bytes 98308
  4.3 0.8 %copy-start.2 = (f32[8]{0:T(128)S(1)}, f32[8]{0:T(128)}, u32[]{:S(2)}) copy-start(f32[8]{0:T(128)} %dt_bias.1) | copy-start | bytes 100
  4.3 0.7 %copy-start.3 = (f32[8]{0:T(128)S(1)}, f32[8]{0:T(128)}, u32[]{:S(2)}) copy-start(f32[8]{0:T(128)} %a_rate.1) | copy-start | bytes 100
  4.3 0.7 %copy-start.4 = (f32[8]{0:T(128)S(1)}, f32[8]{0:T(128)}, u32[]{:S(2)}) copy-start(f32[8]{0:T(128)} %d_skip.1) | copy-start | bytes 100

commit v2 on v1

v2 whole, which is shorter than its diff:
```python
import jax
import jax.numpy as jnp
from jax import lax
from jax.experimental import pallas as pl
from jax.experimental.pallas import tpu as pltpu
from jax.sharding import PartitionSpec as P

MESH = pl.DeviceIdType.MESH
HIGH = lax.Precision.HIGHEST
STEPS = 3
SIDE = 4
CHIPS = 16
PLANE = 32
ROWS = 64
CHUNK = 32
PARTS = 2
PART = CHUNK // PARTS
HALF = 128
TENSOR = 16
GROUPS = 4
NORM_WIDTH = 2048

HOPS = (
    (2, 2), (2, 1), (1, 2), (2, 3), (3, 2), (2, 0), (0, 2), (1, 1),
    (3, 3), (1, 3), (3, 1), (1, 0), (0, 1), (3, 0), (0, 3), (0, 0),
)
OFFSETS = tuple(
    (kc, kx, ky) for kx, ky in HOPS for kc in (0, 1) if (kc, kx, ky) != (0, 0, 0)
)


def dot_nt(a, b, precision=HIGH):
    return lax.dot_general(
        a, b, (((1,), (1,)), ((), ())), precision=precision,
        preferred_element_type=jnp.float32,
    )


def dot_nn(a, b, precision=HIGH):
    return lax.dot_general(
        a, b, (((1,), (0,)), ((), ())), precision=precision,
        preferred_element_type=jnp.float32,
    )


def silu(v):
    return v / (1.0 + jnp.exp(-v))


def column(row_values, same):
    return jnp.sum(jnp.where(same, row_values, 0.0), axis=1, keepdims=True)


def kernel(
    ssm, bcp, bcx, xp, zp, dest, send, w16, wbc, dt_bias, a_rate, d_skip,
    out_s, out_g, out_tot,
    pk, buf, sbuf0, sbuf1, obuf, dxs, decs, mixed, flat, ysend, yrecv,
    sqsend, sqrecv, sidx_v, wbc_v, sidx_s,
    w_sem, pk_ss, pk_rs, s_ss, s_rs, o_ss, o_rs, y_ss, y_rs, q_ss, q_rs, local_sem,
):
    sbufs = (sbuf0, sbuf1)
    d = lax.axis_index("dp")
    z = lax.axis_index("tensor")
    c = d % 2
    q = d // 2
    x = q % SIDE
    y = q // SIDE
    g = z // SIDE
    m = z % SIDE

    def at(offset):
        kc, kx, ky = offset
        cc = (c + kc) % 2
        qq = ((y + ky) % SIDE) * SIDE + (x + kx) % SIDE
        return qq * 2 + cc, qq, cc

    norm_peers = [(d, g * SIDE + (m + i) % SIDE) for i in range(1, SIDE)]

    barrier = pltpu.get_barrier_semaphore()
    signals = 0
    for offset in OFFSETS:
        pl.semaphore_signal(barrier, inc=1, device_id=(at(offset)[0], z), device_id_type=MESH)
        signals += 1
    for peer in norm_peers:
        pl.semaphore_signal(barrier, inc=1, device_id=peer, device_id_type=MESH)
        signals += 1

    w_copies = []
    for h in range(2):
        base = pl.multiple_of(h * 1024 + g * 2 * HALF + c * HALF, HALF)
        w_copies.append(
            pltpu.make_async_copy(wbc.at[:, pl.ds(base, HALF)], wbc_v.at[h], w_sem.at[h])
        )
        w_copies[h].start()

    def fill(qq, _):
        for cc in range(2):
            p = qq * 2 + cc
            for j in range(2):
                for h in range(2):
                    pk[p, j * 2 + h] = bcp[cc, j, h]
                    pk[p, j * 2 + h, 6:7, :] = xp[qq, j : j + 1, HALF * h : HALF * (h + 1)]
            pk[p, 4] = bcx[p]
        return 0

    lax.fori_loop(0, CHIPS, fill, 0)
    pl.semaphore_wait(barrier, signals)

    def lines(device):
        return pl.ds(pl.multiple_of(device * 8, 8), 8)

    def small_copy(p, source):
        return pltpu.make_async_remote_copy(
            src_ref=pk.at[p], dst_ref=buf.at[:, lines(source)],
            send_sem=pk_ss.at[p], recv_sem=pk_rs.at[source],
            device_id=(p, z), device_id_type=MESH,
        )

    def slab(qq, cc, part):
        return (
            slice(None),
            pl.ds(pl.multiple_of(qq * CHUNK + part * PART, PART), PART),
            pl.ds(pl.multiple_of(cc * HALF, HALF), HALF),
        )

    def state_copy(p, qq, cc, part, source):
        return pltpu.make_async_remote_copy(
            src_ref=ssm.at[slab(qq, cc, part)],
            dst_ref=sbufs[part].at[:, source],
            send_sem=s_ss.at[part, p], recv_sem=s_rs.at[part, source],
            device_id=(p, z), device_id_type=MESH,
        )

    own_small = pltpu.make_async_copy(pk.at[d], buf.at[:, lines(d)], local_sem.at[0])
    own_states = [
        pltpu.make_async_copy(
            ssm.at[slab(q, c, part)], sbufs[part].at[:, d], local_sem.at[1 + part]
        )
        for part in range(PARTS)
    ]
    for offset in OFFSETS:
        small_copy(at(offset)[0], d).start()
    own_small.start()
    for part in range(PARTS):
        for offset in OFFSETS:
            p, qq, cc = at(offset)
            state_copy(p, qq, cc, part, d).start()
        own_states[part].start()

    down = lax.broadcasted_iota(jnp.int32, (ROWS, ROWS), 0)
    across = lax.broadcasted_iota(jnp.int32, (ROWS, ROWS), 1)
    same = down == across
    eye = same.astype(jnp.float32)
    moves = []
    picks = []
    for t in range(STEPS):
        dest_row = jnp.concatenate([dest[t : t + 1, :]] * 2, axis=1)
        send_row = jnp.concatenate([send[t : t + 1, :]] * 2, axis=1)
        send_col = jnp.sum(jnp.where(same, send_row, 0), axis=1, keepdims=True)
        arrives = (dest_row == down % PLANE) & (send_row == across // PLANE)
        moved = send_col == down // PLANE
        picks.append((moved & arrives) | (jnp.logical_not(moved) & same))
        moves.append(picks[t].astype(jnp.float32).astype(jnp.bfloat16))
    place2 = moves[2].astype(jnp.float32)
    place1 = dot_nn(moves[2], moves[1], None)
    place0 = dot_nn(place1.astype(jnp.bfloat16), moves[0], None)
    source = jnp.sum(jnp.where(picks[2], across, 0), axis=1, keepdims=True)
    for t in (1, 0):
        before = jnp.sum(jnp.where(picks[t], across, 0), axis=1, keepdims=True)
        before = jnp.sum(jnp.where(same, before, 0), axis=0, keepdims=True)
        source = jnp.sum(jnp.where(across == source, before, 0), axis=1, keepdims=True)
    source = jnp.sum(jnp.where(same, source, 0), axis=0, keepdims=True)
    source = jnp.minimum(jnp.maximum(source, 0), ROWS - 1)
    upper = (source >= PLANE).astype(jnp.int32)
    sidx_v[...] = jnp.zeros((8, HALF), jnp.int32)
    sidx_v[0:1, 0:ROWS] = upper
    sidx_v[1:2, 0:ROWS] = source - upper * PLANE
    to_scalar = pltpu.make_async_copy(sidx_v, sidx_s, local_sem.at[3])
    to_scalar.start()
    places = (place1, place2, eye)

    own_small.wait()
    for offset in OFFSETS:
        p = at(offset)[0]
        small_copy(p, p).wait_recv()

    def entry(e):
        return jnp.concatenate(
            [
                jnp.concatenate(
                    [buf[j * 2 + h, pl.ds(e, PLANE, stride=8), :] for j in range(2)], axis=0
                )
                for h in range(2)
            ],
            axis=1,
        )

    def entry_all(e):
        both = buf[4, pl.ds(e, PLANE, stride=8), :]
        return jnp.concatenate([both[:, : HALF // 2], both[:, HALF // 2 :]], axis=0)

    packed = entry(6)
    turned = jnp.transpose(packed)
    first = dot_nt(turned, place0)
    later = (dot_nt(turned, place1), dot_nt(turned, place2), turned)
    window = [first[CHUNK * k : CHUNK * (k + 1)] for k in range(3)]
    pick = (
        lax.broadcasted_iota(jnp.int32, (CHUNK, HALF), 0)
        == lax.broadcasted_iota(jnp.int32, (CHUNK, HALF), 1)
    ).astype(jnp.float32)
    weights = dot_nt(pick, w16[q])
    head = q // 2
    bias = dt_bias[head]
    rate = a_rate[head]
    skip = jnp.where(c == 0, d_skip[head], 0.0)
    live_cols = []
    skipped = []
    for t in range(STEPS):
        new = later[t][96 + CHUNK * t : 96 + CHUNK * (t + 1)]
        raw = later[t][192 + t : 193 + t] + bias
        live = later[t][195 + t : 196 + t]
        delta = jnp.maximum(raw, 0.0) + jnp.log1p(jnp.exp(-jnp.abs(raw)))
        decay = jnp.exp(-delta * rate)
        mixed_x = silu(
            window[0] * weights[:, 0:1]
            + window[1] * weights[:, 1:2]
            + window[2] * weights[:, 2:3]
            + new * weights[:, 3:4]
        )
        on = jnp.broadcast_to(live, (CHUNK, ROWS)) > 0.5
        dxs[t, :, 0:ROWS] = jnp.where(on, delta * mixed_x, 0.0)
        decs[t, :, 0:ROWS] = jnp.broadcast_to(
            jnp.where(live > 0.5, decay, 1.0), (8, ROWS)
        )
        skipped.append(skip * mixed_x)
        window = [
            jnp.where(on, window[1], window[0]),
            jnp.where(on, window[2], window[1]),
            jnp.where(on, new, window[2]),
        ]
        live_cols.append(column(live, same))

    window_bc = [dot_nn(place0, entry(e)) for e in range(3)]
    for copy in w_copies:
        copy.wait()
    w_bc = jnp.concatenate([wbc_v[0], wbc_v[1]], axis=1)
    window_all = [dot_nn(place0, entry_all(e)) for e in range(3)]
    for t in range(STEPS):
        new = entry(3 + t)
        if t < 2:
            new = dot_nn(places[t], new)
        both = silu(
            window_bc[0] * w_bc[0:1]
            + window_bc[1] * w_bc[1:2]
            + window_bc[2] * w_bc[2:3]
            + new * w_bc[3:4]
        )
        mixed[t, 0] = both[:, :HALF]
        mixed[t, 1] = both[:, HALF:]
        if t < 2:
            on = jnp.broadcast_to(live_cols[t], (ROWS, 2 * HALF)) > 0.5
            window_bc = [
                jnp.where(on, window_bc[1], window_bc[0]),
                jnp.where(on, window_bc[2], window_bc[1]),
                jnp.where(on, new, window_bc[2]),
            ]
        new = entry_all(3 + t)
        if t < 2:
            new = dot_nn(places[t], new)
        on = jnp.broadcast_to(live_cols[t], (ROWS, HALF // 2)) > 0.5
        window_all = [
            jnp.where(on, window_all[1], window_all[0]),
            jnp.where(on, window_all[2], window_all[1]),
            jnp.where(on, new, window_all[2]),
        ]

    def final_copy(p, part, source):
        return pltpu.make_async_remote_copy(
            src_ref=obuf.at[part, :, p], dst_ref=out_s.at[slab(source // 2, source % 2, part)],
            send_sem=o_ss.at[part, p], recv_sem=o_rs.at[part, source],
            device_id=(p, z), device_id_type=MESH,
        )

    own_finals = [
        pltpu.make_async_copy(
            obuf.at[part, :, d], out_s.at[slab(q, c, part)], local_sem.at[4 + part]
        )
        for part in range(PARTS)
    ]
    lane = lax.broadcasted_iota(jnp.int32, (PART, HALF), 1)
    lane8 = lax.broadcasted_iota(jnp.int32, (8, HALF), 1)
    zero = jnp.zeros((PART, HALF), jnp.float32)
    to_scalar.wait()
    reads = []

    def advance_part(part):
        def advance(j, dd, ys):
            f = j * PLANE + dd
            state = sbufs[part][sidx_s[0, f], sidx_s[1, f]].reshape(PART // 8, 8, HALF)
            here = lane == f
            here8 = lane8 == f
            out = []
            for t in range(STEPS):
                dx_all = dxs[t, part * PART : (part + 1) * PART, :]
                dx = jnp.sum(jnp.where(here, dx_all, 0.0), axis=1, keepdims=True)
                dec = jnp.sum(jnp.where(here8, decs[t], 0.0), axis=1, keepdims=True)
                b_row = mixed[t, 0, pl.ds(f, 1), :]
                c_row = mixed[t, 1, pl.ds(f, 1), :]
                state = state * dec[None] + (dx * b_row).reshape(PART // 8, 8, HALF)
                read = jnp.sum(state.reshape(PART, HALF) * c_row, axis=1, keepdims=True)
                out.append(jnp.where(here, read, ys[t]))
            obuf[part, j, dd] = state.reshape(PART, HALF)
            return tuple(out)

        def advance_some(i, ys):
            for k in range(2):
                for j in range(2):
                    ys = advance(j, i * 2 + k, ys)
            return ys

        return lax.fori_loop(0, PLANE // 2, advance_some, (zero,) * STEPS)

    for part in range(PARTS):
        own_states[part].wait()
        for offset in OFFSETS:
            p, qq, cc = at(offset)
            state_copy(p, qq, cc, part, p).wait_recv()
        reads.append(advance_part(part))
        if part < PARTS - 1:
            for offset in OFFSETS:
                final_copy(at(offset)[0], part, d).start()
            own_finals[part].start()

    pieces = [None] * 6
    for t in range(STEPS):
        read = jnp.concatenate([part[t][:, 0:ROWS] for part in reads], axis=0)
        read = read + skipped[t]
        back = eye if t == 2 else dot_nt(eye, places[t])
        pieces[t] = dot_nt(back, read)
        pieces[3 + t] = dot_nt(eye, window[t])
    for n in range(6):
        lo = CHUNK * (n % 4)
        flat[n // 4, :, lo : lo + CHUNK] = pieces[n]
    for n in range(3):
        lo = (HALF // 2) * ((n + 1) % 2)
        flat[1 + (n + 1) // 2, :, lo : lo + HALF // 2] = window_all[n]

    def spread_rows(dd, _):
        for j in range(2):
            for n in range(3):
                ysend[dd, j : j + 1, HALF * n : HALF * (n + 1)] = flat[
                    n, pl.ds(j * PLANE + dd, 1), :
                ]
        return 0

    lax.fori_loop(0, PLANE, spread_rows, 0)

    def read_copy(p, source):
        return pltpu.make_async_remote_copy(
            src_ref=ysend.at[p], dst_ref=yrecv.at[source],
            send_sem=y_ss.at[p], recv_sem=y_rs.at[source],
            device_id=(p, z), device_id_type=MESH,
        )

    own_read = pltpu.make_async_copy(ysend.at[d], yrecv.at[d], local_sem.at[6])
    for offset in OFFSETS:
        read_copy(at(offset)[0], d).start()
    own_read.start()
    for offset in OFFSETS:
        final_copy(at(offset)[0], PARTS - 1, d).start()
    own_finals[PARTS - 1].start()

    own_read.wait()
    for offset in OFFSETS:
        p = at(offset)[0]
        read_copy(p, p).wait_recv()
    lane2 = lax.broadcasted_iota(jnp.int32, (2, 2 * HALF), 1)
    total = jnp.zeros((2, 2 * HALF), jnp.float32)
    for qq in range(CHIPS):
        read = yrecv[2 * qq, :, 0 : 2 * HALF]
        other = yrecv[2 * qq + 1, :, 0 : 2 * HALF]
        read = read + jnp.where(lane2 < 96, other, 0.0)
        gated = read * silu(zp[qq])
        out_g[qq * 2, :, 0 : 2 * HALF] = jnp.where(lane2 < 96, gated, read)
        out_g[qq * 2 + 1, :, 0 : 2 * HALF] = other
        for cc in range(2):
            out_g[qq * 2 + cc, :, 2 * HALF :] = yrecv[qq * 2 + cc, :, 2 * HALF :]
        total = total + gated * gated
    fold = (
        lax.broadcasted_iota(jnp.int32, (2 * HALF, HALF), 0) // CHUNK
        == lax.broadcasted_iota(jnp.int32, (2 * HALF, HALF), 1)
    ).astype(jnp.float32)
    sqsend[...] = jnp.zeros((8, HALF), jnp.float32)
    sqsend[0:2, :] = dot_nn(total, fold)
    sq_copies = []
    for n, peer in enumerate(norm_peers):
        copy = pltpu.make_async_remote_copy(
            src_ref=sqsend, dst_ref=sqrecv.at[n],
            send_sem=q_ss.at[n], recv_sem=q_rs.at[n],
            device_id=peer, device_id_type=MESH,
        )
        copy.start()
        sq_copies.append(copy)
    for copy in sq_copies:
        copy.wait()
    out_tot[...] = sqsend[...] + sqrecv[0] + sqrecv[1] + sqrecv[2]

    for part in range(PARTS):
        own_finals[part].wait()
        for offset in OFFSETS:
            p = at(offset)[0]
            final_copy(p, part, p).wait_recv()
    for offset in OFFSETS:
        p, qq, cc = at(offset)
        small_copy(p, d).wait_send()
        read_copy(p, d).wait_send()
        for part in range(PARTS):
            state_copy(p, qq, cc, part, d).wait_send()
            final_copy(p, part, d).wait_send()


def local(
    ssm_state, conv_x, conv_bc, x_in, bc_in, z_in, dt_in, conv_w_x, conv_w_bc,
    dt_bias, a_rate, d_skip, norm_gain, send_slot, dest_group, active,
):
    f32 = jnp.float32
    g = lax.axis_index("tensor") // SIDE

    bc_all = jnp.concatenate([conv_bc, jnp.swapaxes(bc_in, 0, 1).astype(f32)], axis=1)
    bcx = jnp.transpose(bc_all.reshape(2, 6, PLANE, HALF // 2), (2, 1, 0, 3))
    bcx = jnp.pad(bcx.reshape(PLANE, 6, HALF), ((0, 0), (0, 2), (0, 0)))
    bc_all = lax.dynamic_index_in_dim(
        bc_all.reshape(2, 6, 2, GROUPS, 2, HALF), g, 3, keepdims=False
    )
    bcp = jnp.transpose(bc_all, (3, 0, 2, 1, 4))
    bcp = jnp.pad(bcp, ((0, 0),) * 3 + ((0, 2), (0, 0)))

    x_all = jnp.concatenate([conv_x, jnp.swapaxes(x_in, 0, 1).astype(f32)], axis=1)
    x_all = jnp.transpose(x_all.reshape(2, 6, CHIPS, CHUNK), (2, 0, 1, 3))
    dt_all = jnp.repeat(jnp.transpose(dt_in.astype(f32), (2, 1, 0)), 2, axis=0)
    live = jnp.broadcast_to(jnp.transpose(active).astype(f32)[None], (CHIPS, 2, STEPS))
    xp = jnp.concatenate(
        [x_all.reshape(CHIPS, 2, 192), dt_all, live, jnp.zeros((CHIPS, 2, 58), f32)],
        axis=2,
    )
    zp = jnp.transpose(z_in.astype(f32).reshape(STEPS, 2, CHIPS, CHUNK), (2, 1, 0, 3))
    zp = jnp.pad(zp.reshape(CHIPS, 2, 96), ((0, 0), (0, 0), (0, 160)))
    w16 = jnp.transpose(conv_w_x.reshape(4, CHIPS, CHUNK), (1, 0, 2))
    w16 = jnp.pad(w16, ((0, 0), (0, 4), (0, HALF - CHUNK)))

    vmem = pl.BlockSpec(memory_space=pltpu.VMEM)
    smem = pl.BlockSpec(memory_space=pltpu.SMEM)
    hbm = pl.BlockSpec(memory_space=pl.ANY)
    dma = pltpu.SemaphoreType.DMA
    out_s, out_g, out_tot = pl.pallas_call(
        kernel,
        out_shape=(
            jax.ShapeDtypeStruct((2, 512, 256), f32),
            jax.ShapeDtypeStruct((PLANE, 2, 384), f32),
            jax.ShapeDtypeStruct((8, HALF), f32),
        ),
        in_specs=[hbm] + [vmem] * 7 + [hbm] + [smem] * 3,
        out_specs=(hbm, vmem, vmem),
        scratch_shapes=[
            pltpu.VMEM((PLANE, 5, 8, HALF), f32),
            pltpu.VMEM((5, PLANE * 8, HALF), f32),
            pltpu.VMEM((2, PLANE, PART, HALF), f32),
            pltpu.VMEM((2, PLANE, PART, HALF), f32),
            pltpu.VMEM((PARTS, 2, PLANE, PART, HALF), f32),
            pltpu.VMEM((STEPS, CHUNK, HALF), f32),
            pltpu.VMEM((STEPS, 8, HALF), f32),
            pltpu.VMEM((STEPS, 2, ROWS, HALF), f32),
            pltpu.VMEM((3, ROWS, HALF), f32),
            pltpu.VMEM((PLANE, 2, 384), f32),
            pltpu.VMEM((PLANE, 2, 384), f32),
            pltpu.VMEM((8, HALF), f32),
            pltpu.VMEM((3, 8, HALF), f32),
            pltpu.VMEM((8, HALF), jnp.int32),
            pltpu.VMEM((2, 4, HALF), f32),
            pltpu.SMEM((8, HALF), jnp.int32),
            dma((2,)),
            dma((PLANE,)), dma((PLANE,)),
            dma((PARTS, PLANE)), dma((PARTS, PLANE)),
            dma((PARTS, PLANE)), dma((PARTS, PLANE)),
            dma((PLANE,)), dma((PLANE,)),
            dma((4,)), dma((4,)),
            dma((8,)),
        ],
        compiler_params=pltpu.CompilerParams(
            collective_id=0, has_side_effects=True, vmem_limit_bytes=48 * 2**20
        ),
    )(
        ssm_state.reshape(2, 512, 256), bcp, bcx, xp, zp, dest_group, send_slot, w16,
        conv_w_bc, dt_bias, a_rate, d_skip,
    )

    factor = lax.rsqrt(out_tot[0:2, 0:STEPS] / NORM_WIDTH + 1e-05)
    packed = out_g.reshape(CHIPS, 2, 2, 384)[:, 0, :, 0:192].reshape(CHIPS, 2, 6, CHUNK)
    normed = (
        packed[:, :, 0:3] * factor[None, :, :, None]
        * norm_gain.reshape(CHIPS, 1, 1, CHUNK)
    )
    normed = jnp.where(jnp.transpose(active)[None, :, :, None] > 0, normed, 0.0)
    mixer = jnp.transpose(normed.astype(jnp.bfloat16), (2, 1, 0, 3)).reshape(STEPS, 2, 512)
    final_x = jnp.transpose(packed[:, :, 3:6], (1, 2, 0, 3)).reshape(2, 3, 512)
    final_bc = out_g[:, :, 192:].reshape(PLANE, 2, 3, HALF // 2)
    final_bc = jnp.transpose(final_bc, (1, 2, 0, 3)).reshape(2, 3, 2048)
    return mixer, out_s.reshape(ssm_state.shape), final_x, final_bc


def solution(mesh):
    return jax.shard_map(
        local,
        mesh=mesh,
        in_specs=(
            P("dp", "tensor", None, None),
            P("dp", None, "tensor"),
            P("dp", None, None),
            P(None, "dp", "tensor"),
            P(None, "dp", None),
            P(None, "dp", "tensor"),
            P(None, "dp", "tensor"),
            P(None, "tensor"),
            P(),
            P("tensor"),
            P("tensor"),
            P("tensor"),
            P("tensor"),
            P(),
            P(),
            P(None, "dp"),
        ),
        out_specs=(
            P(None, "dp", "tensor"),
            P("dp", "tensor", None, None),
            P("dp", None, "tensor"),
            P("dp", None, None),
        ),
        check_vma=False,
    )
```

time: 69.1 us -> 60.7 us (0.88)
  Pallas kernels: 60.5 us -> 49.1 us
  local copies, waits for them, and re-layouts: 7.03 us -> 9.98 us
    pallas_call x1, Pallas kernels: 60.5 us -> 49.1 us  [local(): pl.pallas_call(kernel, out_shape=(jax.ShapeDtypeStruct((2, 512, 256), f32...]
    unnamed x34 -> x36, local copies, waits for them, and re-layouts: 3.53 us -> 6.07 us
where the time goes in v2:
time: 60.7 us; the launch traced here: 60.3 us
  Pallas kernels  49.1 us (81%)
  local copies, waits for them, and re-layouts  9.98 us (16%)
  between operations  0.96 us (2%)
    pallas_call x1, Pallas kernels, local(): pl.pallas_call(kernel, out_shape=(jax.ShapeDtypeStruct((2, 512, 256), f32...  49.1 us
    unnamed x36, local copies, waits for them, and re-layouts  6.07 us

profile of v2, /device:TPU:1, one launch (start us, length us, event | category | flops | bytes accessed | tf_op | source)
XLA Modules:
  0.0 60.3 jit_solution(2741487107088800919)
XLA Ops:
  0.7 0.7 %copy-done.8 = bf16[3,2,2048]{2,1,0:T(2,128)(2,1)S(1)} copy-done((bf16[3,2,2048]{2,1,0:T(2,128)(2,1)S(1)}, bf16[3,2,2048]{2,1,0:T(2,128)(2,1)}, u32[]{:S(2)}) %copy-start.8) | copy-done | bytes 24600
  1.5 0.1 reshape.65
  1.7 0.2 reshape.66
  1.9 0.2 copy.64
  2.0 0.2 reshape.67
  2.3 0.3 copy-done.11
  2.6 0.1 reshape.68
  2.8 0.1 reshape.69
  2.9 0.6 %copy-done.14 = bf16[3,2,8]{2,1,0:T(2,128)(2,1)S(1)} copy-done((bf16[3,2,8]{2,1,0:T(2,128)(2,1)S(1)}, bf16[3,2,8]{2,1,0:T(2,128)(2,1)}, u32[]{:S(2)}) %copy-start.14) | copy-done | bytes 120
  3.6 0.1 copy.58
  3.7 0.7 %copy-done.15 = s32[3,2]{0,1:T(2,128)S(1)} copy-done((s32[3,2]{0,1:T(2,128)S(1)}, s32[3,2]{0,1:T(2,128)}, u32[]{:S(2)}) %copy-start.15) | copy-done | bytes 48
  4.4 0.1 maximum_maximum_fusion.xp
  4.5 0.6 copy-done.10
  5.3 0.7 %copy-done.12 = bf16[3,2,512]{2,1,0:T(2,128)(2,1)S(1)} copy-done((bf16[3,2,512]{2,1,0:T(2,128)(2,1)S(1)}, bf16[3,2,512]{2,1,0:T(2,128)(2,1)}, u32[]{:S(2)}) %copy-start.12) | copy-done | bytes 6168
  6.2 0.7 %copy-done.1 = f32[4,2048]{1,0:T(4,128)S(1)} copy-done((f32[4,2048]{1,0:T(4,128)S(1)}, f32[4,2048]{1,0:T(4,128)}, u32[]{:S(2)}) %copy-start.1) | copy-done | bytes 32792
  6.9 49.1 %shard_map.183 = (f32[2,512,256]{2,1,0:T(8,128)S(1)}, f32[32,2,384]{2,1,0:T(2,128)S(1)}, f32[8,128]{1,0:T(8,128)S(1)}) custom-call(f32[2,512,256]{2,1,0:T(8,128)S(1)} %bitcast.64, f32[2,2,2,8,128]{4,3,2,1,0:T(8,128)S(1)} %pad.18.bcp, f32[32,8,128]{2,1,0:T(8,128)S(1)} %pad.19.bcx, f32[16,2,256]{2,1,0:T(2,128)S(1)} %maximum_maximum_fusion.xp, ...), custom_call_target="tpu_custom_call" | custom-call | tf_op jit(solution)/shard_map/pallas_call | solution.py:455
  56.0 0.1 slice.19
  56.1 0.1 reshape.78
  56.3 0.7 %reshape.79 = f32[2,3,2048]{2,0,1:T(2,128)} reshape(f32[2,3,32,64]{3,2,0,1:T(8,128)S(1)} %copy.54) | data formatting | bytes 98304 | tf_op jit(solution)/shard_map/reshape | solution.py:507
  57.1 0.7 %copy-done.13 = f32[512]{0:T(512)S(1)} copy-done((f32[512]{0:T(512)S(1)}, f32[512]{0:T(512)}, u32[]{:S(2)}) %copy-start.13) | copy-done | bytes 2072
  57.8 0.1 slice_bitcast_fusion
  58.0 0.7 %reshape.77 = f32[2,3,512]{2,0,1:T(2,128)} reshape(f32[2,3,16,32]{3,2,0,1:T(8,128)S(1)} %copy.52) | data formatting | bytes 24576 | tf_op jit(solution)/shard_map/reshape | solution.py:505
  58.7 0.7 %reshape.75 = bf16[3,2,512]{2,1,0:T(2,128)(2,1)} reshape(bf16[3,2,16,32]{3,2,1,0:T(8,128)(2,1)S(1)} %copy.51) | data formatting | bytes 12288 | tf_op jit(solution)/shard_map/reshape | solution.py:504
  59.3 1.0 %copy.70 = f32[2,8,64,256]{3,2,1,0:T(8,128)} copy(f32[2,8,64,256]{3,2,1,0:T(8,128)S(1)} %bitcast.65) | data formatting | bytes 2097152
  (59 shorter events, 1.1 us)
Async XLA Ops:
  0.6 0.7 %copy-start.8 = (bf16[3,2,2048]{2,1,0:T(2,128)(2,1)S(1)}, bf16[3,2,2048]{2,1,0:T(2,128)(2,1)}, u32[]{:S(2)}) copy-start(bf16[3,2,2048]{2,1,0:T(2,128)(2,1)} %param.20) | copy-start | bytes 73732
  0.6 0.8 %copy-start.7 = (f32[2,3,2048]{2,0,1:T(2,128)S(1)}, f32[2,3,2048]{2,0,1:T(2,128)}, u32[]{:S(2)}) copy-start(f32[2,3,2048]{2,0,1:T(2,128)} %param.18) | copy-start | bytes 147460
  1.9 0.7 %copy-start.11 = (bf16[3,2,512]{2,1,0:T(2,128)(2,1)S(1)}, bf16[3,2,512]{2,1,0:T(2,128)(2,1)}, u32[]{:S(2)}) copy-start(bf16[3,2,512]{2,1,0:T(2,128)(2,1)} %param.19) | copy-start | bytes 18436
  1.9 0.7 %copy-start.9 = (f32[2,3,512]{2,0,1:T(2,128)S(1)}, f32[2,3,512]{2,0,1:T(2,128)}, u32[]{:S(2)}) copy-start(f32[2,3,512]{2,0,1:T(2,128)} %param.17) | copy-start | bytes 36868
  2.0 4.2 %copy-start = (f32[2,8,64,256]{3,2,1,0:T(8,128)S(1)}, f32[2,8,64,256]{3,2,1,0:T(8,128)}, u32[]{:S(2)}) copy-start(f32[2,8,64,256]{3,2,1,0:T(8,128)} %param.16) | copy-start | bytes 3145732
  2.9 0.7 %copy-start.14 = (bf16[3,2,8]{2,1,0:T(2,128)(2,1)S(1)}, bf16[3,2,8]{2,1,0:T(2,128)(2,1)}, u32[]{:S(2)}) copy-start(bf16[3,2,8]{2,1,0:T(2,128)(2,1)} %param.22) | copy-start | bytes 292
  3.7 0.7 %copy-start.15 = (s32[3,2]{0,1:T(2,128)S(1)}, s32[3,2]{0,1:T(2,128)}, u32[]{:S(2)}) copy-start(s32[3,2]{0,1:T(2,128)} %param.31) | copy-start | bytes 76
  4.4 0.7 %copy-start.10 = (f32[4,512]{1,0:T(4,128)S(1)}, f32[4,512]{1,0:T(4,128)}, u32[]{:S(2)}) copy-start(f32[4,512]{1,0:T(4,128)} %param.23) | copy-start | bytes 24580
  5.2 0.7 %copy-start.12 = (bf16[3,2,512]{2,1,0:T(2,128)(2,1)S(1)}, bf16[3,2,512]{2,1,0:T(2,128)(2,1)}, u32[]{:S(2)}) copy-start(bf16[3,2,512]{2,1,0:T(2,128)(2,1)} %param.21) | copy-start | bytes 18436
  6.1 0.8 %copy-start.1 = (f32[4,2048]{1,0:T(4,128)S(1)}, f32[4,2048]{1,0:T(4,128)}, u32[]{:S(2)}) copy-start(f32[4,2048]{1,0:T(4,128)} %wbc.1) | copy-start | bytes 98308
  6.1 0.7 %copy-start.2 = (s32[3,32]{1,0:T(4,128)S(1)}, s32[3,32]{1,0:T(4,128)}, u32[]{:S(2)}) copy-start(s32[3,32]{1,0:T(4,128)} %dest.1) | copy-start | bytes 1156
  6.2 0.7 %copy-start.3 = (s32[3,32]{1,0:T(4,128)S(1)}, s32[3,32]{1,0:T(4,128)}, u32[]{:S(2)}) copy-start(s32[3,32]{1,0:T(4,128)} %send.1) | copy-start | bytes 1156
  6.2 0.7 %copy-start.4 = (f32[8]{0:T(128)S(1)}, f32[8]{0:T(128)}, u32[]{:S(2)}) copy-start(f32[8]{0:T(128)} %dt_bias.1) | copy-start | bytes 100
  6.2 0.7 %copy-start.5 = (f32[8]{0:T(128)S(1)}, f32[8]{0:T(128)}, u32[]{:S(2)}) copy-start(f32[8]{0:T(128)} %a_rate.1) | copy-start | bytes 100
  6.2 0.7 %copy-start.6 = (f32[8]{0:T(128)S(1)}, f32[8]{0:T(128)}, u32[]{:S(2)}) copy-start(f32[8]{0:T(128)} %d_skip.1) | copy-start | bytes 100
  57.1 0.7 %copy-start.13 = (f32[512]{0:T(512)S(1)}, f32[512]{0:T(512)}, u32[]{:S(2)}) copy-start(f32[512]{0:T(512)} %param.28) | copy-start | bytes 6148

commit v3 on v2

--- a/solution.py
+++ b/solution.py
@@ -13,6 +13,8 @@
 PLANE = 32
 ROWS = 64
 CHUNK = 32
+FIXED = 15
+VMEM_BYTES = 63 * 2**20
 PARTS = 2
 PART = CHUNK // PARTS
 HALF = 128
@@ -43,6 +45,10 @@
     )
 
 
+def stack4(v):
+    return jnp.concatenate([v[:, HALF * a : HALF * (a + 1)] for a in range(4)], axis=0)
+
+
 def silu(v):
     return v / (1.0 + jnp.exp(-v))
 
@@ -52,11 +58,20 @@
 
 
 def kernel(
-    ssm, bcp, bcx, xp, zp, dest, send, w16, wbc, dt_bias, a_rate, d_skip,
-    out_s, out_g, out_tot,
+    ssm, *refs,
+):
+    given, refs = refs[:FIXED], refs[FIXED:]
+    outs, held, refs = refs[:4], refs[4 : 4 + FIXED], refs[4 + FIXED :]
+    run(ssm, *held, *outs, given, held, *refs)
+
+
+def run(
+    ssm, cx, xin, cbc, bcin, zin, dtin, wx, wbc, gain, dest, send,
+    active, dt_bias, a_rate, d_skip,
+    out_s, out_m, out_x, out_bc, given, held, in_sem,
     pk, buf, sbuf0, sbuf1, obuf, dxs, decs, mixed, flat, ysend, yrecv,
-    sqsend, sqrecv, sidx_v, wbc_v, sidx_s,
-    w_sem, pk_ss, pk_rs, s_ss, s_rs, o_ss, o_rs, y_ss, y_rs, q_ss, q_rs, local_sem,
+    sqsend, sqrecv, sidx_v, bcf, model, extra, sidx_s,
+    pk_ss, pk_rs, s_ss, s_rs, o_ss, o_rs, y_ss, y_rs, q_ss, q_rs, local_sem,
 ):
     sbufs = (sbuf0, sbuf1)
     d = lax.axis_index("dp")
@@ -76,6 +91,12 @@
 
     norm_peers = [(d, g * SIDE + (m + i) % SIDE) for i in range(1, SIDE)]
 
+    loads = [
+        pltpu.make_async_copy(source, target, in_sem.at[n])
+        for n, (source, target) in enumerate(zip(given, held))
+    ]
+    for copy in loads:
+        copy.start()
     barrier = pltpu.get_barrier_semaphore()
     signals = 0
     for offset in OFFSETS:
@@ -85,25 +106,62 @@
         pl.semaphore_signal(barrier, inc=1, device_id=peer, device_id_type=MESH)
         signals += 1
 
-    w_copies = []
-    for h in range(2):
-        base = pl.multiple_of(h * 1024 + g * 2 * HALF + c * HALF, HALF)
-        w_copies.append(
-            pltpu.make_async_copy(wbc.at[:, pl.ds(base, HALF)], wbc_v.at[h], w_sem.at[h])
-        )
-        w_copies[h].start()
+    for copy in loads:
+        copy.wait()
+    lane8 = lax.broadcasted_iota(jnp.int32, (8, HALF), 1)
+    lane1 = lax.broadcasted_iota(jnp.int32, (1, HALF), 1)
+    for t in range(STEPS):
+        bcf[t] = bcin[t].astype(jnp.float32)
+    extra[...] = jnp.zeros((8, HALF), jnp.float32)
+    for t in range(STEPS):
+        extra[0:2, 8 * t : 8 * t + 8] = dtin[t].astype(jnp.float32)
+    for j in range(2):
+        for t in range(STEPS):
+            extra[j : j + 1, :] = jnp.where(
+                lane1 == 24 + t, active[j, t].astype(jnp.float32), extra[j : j + 1, :]
+            )
+    model[...] = jnp.zeros((2, 4, 8, HALF), jnp.float32)
+    for cc in range(2):
+        for h in range(2):
+            base = pl.multiple_of(h * 1024 + g * 2 * HALF + cc * HALF, HALF)
+            for j in range(2):
+                for e in range(6):
+                    table = cbc if e < 3 else bcf
+                    model[cc, 2 * j + h, e : e + 1, :] = table[
+                        e % 3, j : j + 1, pl.ds(base, HALF)
+                    ]
+        for j in range(2):
+            model[cc, 2 * j, 7:8, :] = extra[j : j + 1, :]
 
     def fill(qq, _):
+        place = pl.ds(pl.multiple_of(qq * HALF, HALF), HALF)
         for cc in range(2):
-            p = qq * 2 + cc
-            for j in range(2):
-                for h in range(2):
-                    pk[p, j * 2 + h] = bcp[cc, j, h]
-                    pk[p, j * 2 + h, 6:7, :] = xp[qq, j : j + 1, HALF * h : HALF * (h + 1)]
-            pk[p, 4] = bcx[p]
+            pk[qq * 2 + cc, 0:4] = model[cc]
+            pk[qq * 2 + cc, 4] = jnp.zeros((8, HALF), jnp.float32)
+        for e in range(6):
+            table = cbc if e < 3 else bcf
+            both = table[e % 3, :, place]
+            turn = pltpu.roll(both, HALF // 2, 1)
+            low = lane1 < HALF // 2
+            pk[qq * 2, 4, e : e + 1, :] = jnp.where(low, both[0:1], turn[1:2])
+            pk[qq * 2 + 1, 4, e : e + 1, :] = jnp.where(low, turn[0:1], both[1:2])
         return 0
 
     lax.fori_loop(0, CHIPS, fill, 0)
+    stacks = [stack4(cx[e]) for e in range(3)]
+    stacks += [stack4(xin[e].astype(jnp.float32)) for e in range(3)]
+    for b in range(4):
+        for h in range(2):
+            row = jnp.zeros((8, HALF), jnp.float32)
+            for e in range(4 * h, min(6, 4 * h + 4)):
+                moved = pltpu.roll(stacks[e], (CHUNK * (e % 4 - b)) % HALF, 1)
+                row = jnp.where(lane8 // CHUNK == e % 4, moved, row)
+            for a in range(4):
+                for j in range(2):
+                    for cc in range(2):
+                        p = 2 * (4 * a + b) + cc
+                        pk[p, 2 * j + h, 6:7, :] = row[2 * a + j : 2 * a + j + 1]
+
     pl.semaphore_wait(barrier, signals)
 
     def lines(device):
@@ -200,15 +258,28 @@
         return jnp.concatenate([both[:, : HALF // 2], both[:, HALF // 2 :]], axis=0)
 
     packed = entry(6)
+    marks = jnp.concatenate(
+        [buf[j * 2, pl.ds(7, PLANE, stride=8), :] for j in range(2)], axis=0
+    )
     turned = jnp.transpose(packed)
-    first = dot_nt(turned, place0)
-    later = (dot_nt(turned, place1), dot_nt(turned, place2), turned)
+    marks = jnp.transpose(marks)[0:CHUNK]
+    first = dot_nt(turned[0:96], place0)
+    fresh_x = []
+    fresh_marks = []
+    for t in range(STEPS):
+        new = turned[96 + CHUNK * t : 96 + CHUNK * (t + 1)]
+        fresh_x.append(new if t == 2 else dot_nt(new, places[t]))
+        fresh_marks.append(marks if t == 2 else dot_nt(marks, places[t]))
     window = [first[CHUNK * k : CHUNK * (k + 1)] for k in range(3)]
     pick = (
-        lax.broadcasted_iota(jnp.int32, (CHUNK, HALF), 0)
+        lax.broadcasted_iota(jnp.int32, (CHUNK, HALF), 0) + CHUNK * (q % 4)
         == lax.broadcasted_iota(jnp.int32, (CHUNK, HALF), 1)
     ).astype(jnp.float32)
-    weights = dot_nt(pick, w16[q])
+    quarter = wx[:, pl.ds(pl.multiple_of(q // 4 * HALF, HALF), HALF)]
+    weights = dot_nt(
+        pick, jnp.concatenate([quarter, jnp.zeros((4, HALF), jnp.float32)], axis=0)
+    )
+    of_head = lax.broadcasted_iota(jnp.int32, (8, ROWS), 0) == q // 2
     head = q // 2
     bias = dt_bias[head]
     rate = a_rate[head]
@@ -216,9 +287,10 @@
     live_cols = []
     skipped = []
     for t in range(STEPS):
-        new = later[t][96 + CHUNK * t : 96 + CHUNK * (t + 1)]
-        raw = later[t][192 + t : 193 + t] + bias
-        live = later[t][195 + t : 196 + t]
+        new = fresh_x[t]
+        raw = jnp.where(of_head, fresh_marks[t][8 * t : 8 * t + 8], 0.0)
+        raw = jnp.sum(raw, axis=0, keepdims=True) + bias
+        live = fresh_marks[t][24 + t : 25 + t]
         delta = jnp.maximum(raw, 0.0) + jnp.log1p(jnp.exp(-jnp.abs(raw)))
         decay = jnp.exp(-delta * rate)
         mixed_x = silu(
@@ -241,9 +313,13 @@
         live_cols.append(column(live, same))
 
     window_bc = [dot_nn(place0, entry(e)) for e in range(3)]
-    for copy in w_copies:
-        copy.wait()
-    w_bc = jnp.concatenate([wbc_v[0], wbc_v[1]], axis=1)
+    w_bc = jnp.concatenate(
+        [
+            wbc[:, pl.ds(pl.multiple_of(h * 1024 + g * 2 * HALF + c * HALF, HALF), HALF)]
+            for h in range(2)
+        ],
+        axis=1,
+    )
     window_all = [dot_nn(place0, entry_all(e)) for e in range(3)]
     for t in range(STEPS):
         new = entry(3 + t)
@@ -288,7 +364,6 @@
         for part in range(PARTS)
     ]
     lane = lax.broadcasted_iota(jnp.int32, (PART, HALF), 1)
-    lane8 = lax.broadcasted_iota(jnp.int32, (8, HALF), 1)
     zero = jnp.zeros((PART, HALF), jnp.float32)
     to_scalar.wait()
     reads = []
@@ -374,24 +449,31 @@
     for offset in OFFSETS:
         p = at(offset)[0]
         read_copy(p, p).wait_recv()
-    lane2 = lax.broadcasted_iota(jnp.int32, (2, 2 * HALF), 1)
-    total = jnp.zeros((2, 2 * HALF), jnp.float32)
-    for qq in range(CHIPS):
-        read = yrecv[2 * qq, :, 0 : 2 * HALF]
-        other = yrecv[2 * qq + 1, :, 0 : 2 * HALF]
-        read = read + jnp.where(lane2 < 96, other, 0.0)
-        gated = read * silu(zp[qq])
-        out_g[qq * 2, :, 0 : 2 * HALF] = jnp.where(lane2 < 96, gated, read)
-        out_g[qq * 2 + 1, :, 0 : 2 * HALF] = other
-        for cc in range(2):
-            out_g[qq * 2 + cc, :, 2 * HALF :] = yrecv[qq * 2 + cc, :, 2 * HALF :]
-        total = total + gated * gated
-    fold = (
-        lax.broadcasted_iota(jnp.int32, (2 * HALF, HALF), 0) // CHUNK
-        == lax.broadcasted_iota(jnp.int32, (2 * HALF, HALF), 1)
-    ).astype(jnp.float32)
-    sqsend[...] = jnp.zeros((8, HALF), jnp.float32)
-    sqsend[0:2, :] = dot_nn(total, fold)
+
+    def gather4(h, b, cc):
+        return jnp.concatenate(
+            [
+                yrecv[2 * (4 * a + b) + cc, :, HALF * h : HALF * (h + 1)]
+                for a in range(4)
+            ],
+            axis=0,
+        )
+
+    wide = [jnp.zeros((8, HALF), jnp.float32)] * 6
+    for b in range(4):
+        tiles = [gather4(0, b, 0), gather4(1, b, 0)]
+        summed = tiles[0] + gather4(0, b, 1)
+        for e in range(6):
+            tile = summed if e < 3 else tiles[e // 4]
+            moved = pltpu.roll(tile, (CHUNK * (b - e % 4)) % HALF, 1)
+            wide[e] = jnp.where(lane8 // CHUNK == b, moved, wide[e])
+    gated = []
+    squares = jnp.zeros((8, HALF), jnp.float32)
+    for t in range(STEPS):
+        gated.append(wide[t] * silu(stack4(zin[t].astype(jnp.float32))))
+        part = jnp.sum(gated[t] * gated[t], axis=1, keepdims=True)
+        squares = jnp.where(lane8 == t, part, squares)
+    sqsend[...] = squares
     sq_copies = []
     for n, peer in enumerate(norm_peers):
         copy = pltpu.make_async_remote_copy(
@@ -401,9 +483,35 @@
         )
         copy.start()
         sq_copies.append(copy)
+    low = lane8[0:2] < HALF // 2
+    for a in range(4):
+        for e in range(3):
+            out_x[e, :, HALF * a : HALF * (a + 1)] = wide[3 + e][2 * a : 2 * a + 2]
+    for qq in range(CHIPS):
+        for e in range(3):
+            tile = HALF * (1 + (e + 1) // 2)
+            left = yrecv[2 * qq, :, tile : tile + HALF]
+            right = yrecv[2 * qq + 1, :, tile : tile + HALF]
+            if e == 1:
+                right = pltpu.roll(right, HALF // 2, 1)
+            else:
+                left = pltpu.roll(left, HALF // 2, 1)
+            out_bc[e, :, HALF * qq : HALF * (qq + 1)] = jnp.where(low, left, right)
     for copy in sq_copies:
         copy.wait()
-    out_tot[...] = sqsend[...] + sqrecv[0] + sqrecv[1] + sqrecv[2]
+    total = sqsend[...] + sqrecv[0] + sqrecv[1] + sqrecv[2]
+    even = lax.broadcasted_iota(jnp.int32, (8, HALF), 0) % 2 == 0
+    gains = jnp.concatenate([gain[n // 2 : n // 2 + 1, :] for n in range(8)], axis=0)
+    for t in range(STEPS):
+        col = jnp.sum(jnp.where(lane8 == t, total, 0.0), axis=1, keepdims=True)
+        col = jnp.broadcast_to(col, (8, HALF))
+        of_even = jnp.sum(jnp.where(even, col, 0.0), axis=0, keepdims=True)
+        of_odd = jnp.sum(jnp.where(even, 0.0, col), axis=0, keepdims=True)
+        factor = lax.rsqrt(jnp.where(even, of_even, of_odd) / NORM_WIDTH + 1e-05)
+        on = jnp.where(even, active[0, t], active[1, t]) > 0
+        normed = jnp.where(on, gated[t] * factor * gains, 0.0)
+        for a in range(4):
+            out_m[t, :, HALF * a : HALF * (a + 1)] = normed[2 * a : 2 * a + 2]
 
     for part in range(PARTS):
         own_finals[part].wait()
@@ -419,49 +527,66 @@
             final_copy(p, part, d).wait_send()
 
 
+def finish(*refs):
+    given, outs, held, mixer, sems = refs[:4], refs[4:8], refs[8:12], refs[12], refs[13]
+    loads = [
+        pltpu.make_async_copy(source, target, sems.at[0, n])
+        for n, (source, target) in enumerate(zip(given, held))
+    ]
+    for copy in loads:
+        copy.start()
+    stores = [
+        pltpu.make_async_copy(source, target, sems.at[1, n])
+        for n, (source, target) in enumerate(zip((*held[:3], mixer), outs))
+    ]
+    for n in (1, 2):
+        loads[n].wait()
+        stores[n].start()
+    loads[3].wait()
+    mixer[...] = held[3][...].astype(jnp.bfloat16)
+    stores[3].start()
+    loads[0].wait()
+    stores[0].start()
+    for copy in stores:
+        copy.wait()
+
+
 def local(
     ssm_state, conv_x, conv_bc, x_in, bc_in, z_in, dt_in, conv_w_x, conv_w_bc,
     dt_bias, a_rate, d_skip, norm_gain, send_slot, dest_group, active,
 ):
     f32 = jnp.float32
-    g = lax.axis_index("tensor") // SIDE
-
-    bc_all = jnp.concatenate([conv_bc, jnp.swapaxes(bc_in, 0, 1).astype(f32)], axis=1)
-    bcx = jnp.transpose(bc_all.reshape(2, 6, PLANE, HALF // 2), (2, 1, 0, 3))
-    bcx = jnp.pad(bcx.reshape(PLANE, 6, HALF), ((0, 0), (0, 2), (0, 0)))
-    bc_all = lax.dynamic_index_in_dim(
-        bc_all.reshape(2, 6, 2, GROUPS, 2, HALF), g, 3, keepdims=False
-    )
-    bcp = jnp.transpose(bc_all, (3, 0, 2, 1, 4))
-    bcp = jnp.pad(bcp, ((0, 0),) * 3 + ((0, 2), (0, 0)))
-
-    x_all = jnp.concatenate([conv_x, jnp.swapaxes(x_in, 0, 1).astype(f32)], axis=1)
-    x_all = jnp.transpose(x_all.reshape(2, 6, CHIPS, CHUNK), (2, 0, 1, 3))
-    dt_all = jnp.repeat(jnp.transpose(dt_in.astype(f32), (2, 1, 0)), 2, axis=0)
-    live = jnp.broadcast_to(jnp.transpose(active).astype(f32)[None], (CHIPS, 2, STEPS))
-    xp = jnp.concatenate(
-        [x_all.reshape(CHIPS, 2, 192), dt_all, live, jnp.zeros((CHIPS, 2, 58), f32)],
-        axis=2,
-    )
-    zp = jnp.transpose(z_in.astype(f32).reshape(STEPS, 2, CHIPS, CHUNK), (2, 1, 0, 3))
-    zp = jnp.pad(zp.reshape(CHIPS, 2, 96), ((0, 0), (0, 0), (0, 160)))
-    w16 = jnp.transpose(conv_w_x.reshape(4, CHIPS, CHUNK), (1, 0, 2))
-    w16 = jnp.pad(w16, ((0, 0), (0, 4), (0, HALF - CHUNK)))
-
     vmem = pl.BlockSpec(memory_space=pltpu.VMEM)
-    smem = pl.BlockSpec(memory_space=pltpu.SMEM)
-    hbm = pl.BlockSpec(memory_space=pl.ANY)
+    hbm = pl.BlockSpec(memory_space=pltpu.HBM)
     dma = pltpu.SemaphoreType.DMA
-    out_s, out_g, out_tot = pl.pallas_call(
+    shapes = [
+        jax.ShapeDtypeStruct((2, 512, 256), f32),
+        jax.ShapeDtypeStruct((STEPS, 2, 512), f32),
+        jax.ShapeDtypeStruct((3, 2, 512), f32),
+        jax.ShapeDtypeStruct((3, 2, 2048), f32),
+    ]
+    state, mix, final_x, final_bc = pl.pallas_call(
         kernel,
-        out_shape=(
-            jax.ShapeDtypeStruct((2, 512, 256), f32),
-            jax.ShapeDtypeStruct((PLANE, 2, 384), f32),
-            jax.ShapeDtypeStruct((8, HALF), f32),
-        ),
-        in_specs=[hbm] + [vmem] * 7 + [hbm] + [smem] * 3,
-        out_specs=(hbm, vmem, vmem),
+        out_shape=tuple(shapes),
+        in_specs=[hbm] * (1 + FIXED),
+        out_specs=(hbm, vmem, vmem, vmem),
         scratch_shapes=[
+            pltpu.VMEM((3, 2, 512), f32),
+            pltpu.VMEM((STEPS, 2, 512), jnp.bfloat16),
+            pltpu.VMEM((3, 2, 2048), f32),
+            pltpu.VMEM((STEPS, 2, 2048), jnp.bfloat16),
+            pltpu.VMEM((STEPS, 2, 512), jnp.bfloat16),
+            pltpu.VMEM((STEPS, 2, 8), jnp.bfloat16),
+            pltpu.VMEM((4, 512), f32),
+            pltpu.VMEM((4, 2048), f32),
+            pltpu.VMEM((4, HALF), f32),
+            pltpu.VMEM((STEPS, PLANE), jnp.int32),
+            pltpu.VMEM((STEPS, PLANE), jnp.int32),
+            pltpu.SMEM((2, STEPS), jnp.int32),
+            pltpu.SMEM((8,), f32),
+            pltpu.SMEM((8,), f32),
+            pltpu.SMEM((8,), f32),
+            dma((16,)),
             pltpu.VMEM((PLANE, 5, 8, HALF), f32),
             pltpu.VMEM((5, PLANE * 8, HALF), f32),
             pltpu.VMEM((2, PLANE, PART, HALF), f32),
@@ -476,9 +601,10 @@
             pltpu.VMEM((8, HALF), f32),
             pltpu.VMEM((3, 8, HALF), f32),
             pltpu.VMEM((8, HALF), jnp.int32),
-            pltpu.VMEM((2, 4, HALF), f32),
+            pltpu.VMEM((STEPS, 2, 2048), f32),
+            pltpu.VMEM((2, 4, 8, HALF), f32),
+            pltpu.VMEM((8, HALF), f32),
             pltpu.SMEM((8, HALF), jnp.int32),
-            dma((2,)),
             dma((PLANE,)), dma((PLANE,)),
             dma((PARTS, PLANE)), dma((PARTS, PLANE)),
             dma((PARTS, PLANE)), dma((PARTS, PLANE)),
@@ -487,25 +613,31 @@
             dma((8,)),
         ],
         compiler_params=pltpu.CompilerParams(
-            collective_id=0, has_side_effects=True, vmem_limit_bytes=48 * 2**20
+            collective_id=0, has_side_effects=True, vmem_limit_bytes=VMEM_BYTES
         ),
     )(
-        ssm_state.reshape(2, 512, 256), bcp, bcx, xp, zp, dest_group, send_slot, w16,
-        conv_w_bc, dt_bias, a_rate, d_skip,
-    )
-
-    factor = lax.rsqrt(out_tot[0:2, 0:STEPS] / NORM_WIDTH + 1e-05)
-    packed = out_g.reshape(CHIPS, 2, 2, 384)[:, 0, :, 0:192].reshape(CHIPS, 2, 6, CHUNK)
-    normed = (
-        packed[:, :, 0:3] * factor[None, :, :, None]
-        * norm_gain.reshape(CHIPS, 1, 1, CHUNK)
-    )
-    normed = jnp.where(jnp.transpose(active)[None, :, :, None] > 0, normed, 0.0)
-    mixer = jnp.transpose(normed.astype(jnp.bfloat16), (2, 1, 0, 3)).reshape(STEPS, 2, 512)
-    final_x = jnp.transpose(packed[:, :, 3:6], (1, 2, 0, 3)).reshape(2, 3, 512)
-    final_bc = out_g[:, :, 192:].reshape(PLANE, 2, 3, HALF // 2)
-    final_bc = jnp.transpose(final_bc, (1, 2, 0, 3)).reshape(2, 3, 2048)
-    return mixer, out_s.reshape(ssm_state.shape), final_x, final_bc
+        ssm_state.reshape(2, 512, 256), jnp.swapaxes(conv_x, 0, 1), x_in,
+        jnp.swapaxes(conv_bc, 0, 1), bc_in, z_in, dt_in, conv_w_x, conv_w_bc,
+        norm_gain.reshape(4, HALF), dest_group, send_slot, jnp.transpose(active),
+        dt_bias, a_rate, d_skip,
+    )
+    bits = jax.ShapeDtypeStruct((STEPS, 2, 512), jnp.bfloat16)
+    state, final_x, final_bc, mixer = pl.pallas_call(
+        finish,
+        out_shape=(shapes[0], shapes[2], shapes[3], bits),
+        in_specs=[hbm] * 4,
+        out_specs=(hbm,) * 4,
+        scratch_shapes=[
+            pltpu.VMEM(shapes[n].shape, f32) for n in (0, 2, 3, 1)
+        ] + [pltpu.VMEM(bits.shape, jnp.bfloat16), dma((2, 4))],
+        compiler_params=pltpu.CompilerParams(vmem_limit_bytes=VMEM_BYTES),
+    )(state, final_x, final_bc, mix)
+    return (
+        mixer,
+        state.reshape(ssm_state.shape),
+        jnp.swapaxes(final_x, 0, 1),
+        jnp.swapaxes(final_bc, 0, 1),
+    )
 
 
 def solution(mesh):

time: 60.7 us -> 52.5 us (0.86)
  local copies, waits for them, and re-layouts: 9.98 us -> 0 us
  Pallas kernels: 49.1 us -> 51.6 us
    unnamed x36 -> x0, local copies, waits for them, and re-layouts: 6.07 us -> none
    reshape x19 -> x0, local copies, waits for them, and re-layouts: 3.45 us -> none  [the longest x1 0.72 us: local(): final_bc = jnp.transpose(final_bc, (1, 2, 0, 3)).reshape(2, 3, 2048)]
    pallas_call x1 -> x2, Pallas kernels: 49.1 us -> 51.6 us  [the longest x1 49.3 us: local(): pl.pallas_call(kernel, out_shape=tuple(shapes), in_specs=[hbm] * (1 + FIX...]
where the time goes in v3:
time: 52.5 us; the launch traced here: 52.3 us
  Pallas kernels  51.6 us (98%)
  between operations  0.65 us (1%)
    pallas_call x1, Pallas kernels, local(): pl.pallas_call(kernel, out_shape=tuple(shapes), in_specs=[hbm] * (1 + FIX...  49.3 us
    pallas_call x1, Pallas kernels, local(): pl.pallas_call(finish, out_shape=(shapes[0], shapes[2], shapes[3], bits),...  2.27 us

profile of v3, /device:TPU:1, one launch (start us, length us, event | category | flops | bytes accessed | tf_op | source)
XLA Modules:
  0.0 52.3 jit_solution(165746881795527678)
XLA Ops:
  0.6 49.3 %shard_map.183 = (f32[2,512,256]{2,1,0:T(8,128)}, f32[3,2,512]{2,1,0:T(2,128)}, f32[3,2,512]{2,1,0:T(2,128)}, f32[3,2,2048]{2,1,0:T(2,128)}) custom-call(f32[2,512,256]{2,1,0:T(8,128)} %bitcast.8, f32[3,2,512]{2,1,0:T(2,128)} %bitcast.10, bf16[3,2,512]{2,1,0:T(2,128)(2,1)} %refs_1_.1, f32[3,2,2048]{2,1,0:T(2,128)} %bitcast.9, bf16[3,2,2048]{2,1,0:T(2,128)(2,1)} %refs_3_.1, ...), custom_call_target="tpu_custom_call" | custom-call | tf_op jit(solution)/shard_map/pallas_call | solution.py:568
  50.0 2.3 %shard_map.184 = (f32[2,512,256]{2,1,0:T(8,128)}, f32[3,2,512]{2,1,0:T(2,128)}, f32[3,2,2048]{2,1,0:T(2,128)}, bf16[3,2,512]{2,1,0:T(2,128)(2,1)}) custom-call(f32[2,512,256]{2,1,0:T(8,128)} %get-tuple-element.12.refs_0_, f32[3,2,512]{2,1,0:T(2,128)} %get-tuple-element.13.refs_1_, f32[3,2,2048]{2,1,0:T(2,128)} %get-tuple-element.14.refs_2_, ...), custom_call_target="tpu_custom_call" | custom-call | tf_op jit(solution)/shard_map/pallas_call | solution.py:625

commit v4 on v3

--- a/solution.py
+++ b/solution.py
@@ -14,6 +14,7 @@
 ROWS = 64
 CHUNK = 32
 FIXED = 15
+FEW = 16
 VMEM_BYTES = 63 * 2**20
 PARTS = 2
 PART = CHUNK // PARTS
@@ -69,7 +70,7 @@
     ssm, cx, xin, cbc, bcin, zin, dtin, wx, wbc, gain, dest, send,
     active, dt_bias, a_rate, d_skip,
     out_s, out_m, out_x, out_bc, given, held, in_sem,
-    pk, buf, sbuf0, sbuf1, obuf, dxs, decs, mixed, flat, ysend, yrecv,
+    pk, buf, sbuf0, sbuf1, obuf, dxs, decs, mixed, flat, ysend, yrecv, ends, pushes, fades,
     sqsend, sqrecv, sidx_v, bcf, model, extra, sidx_s,
     pk_ss, pk_rs, s_ss, s_rs, o_ss, o_rs, y_ss, y_rs, q_ss, q_rs, local_sem,
 ):
@@ -114,11 +115,11 @@
         bcf[t] = bcin[t].astype(jnp.float32)
     extra[...] = jnp.zeros((8, HALF), jnp.float32)
     for t in range(STEPS):
-        extra[0:2, 8 * t : 8 * t + 8] = dtin[t].astype(jnp.float32)
+        extra[0:2, 64 + 8 * t : 72 + 8 * t] = dtin[t].astype(jnp.float32)
     for j in range(2):
         for t in range(STEPS):
             extra[j : j + 1, :] = jnp.where(
-                lane1 == 24 + t, active[j, t].astype(jnp.float32), extra[j : j + 1, :]
+                lane1 == 88 + t, active[j, t].astype(jnp.float32), extra[j : j + 1, :]
             )
     model[...] = jnp.zeros((2, 4, 8, HALF), jnp.float32)
     for cc in range(2):
@@ -130,32 +131,33 @@
                     model[cc, 2 * j + h, e : e + 1, :] = table[
                         e % 3, j : j + 1, pl.ds(base, HALF)
                     ]
-        for j in range(2):
-            model[cc, 2 * j, 7:8, :] = extra[j : j + 1, :]
-
-    def fill(qq, _):
-        place = pl.ds(pl.multiple_of(qq * HALF, HALF), HALF)
-        for cc in range(2):
-            pk[qq * 2 + cc, 0:4] = model[cc]
-            pk[qq * 2 + cc, 4] = jnp.zeros((8, HALF), jnp.float32)
-        for e in range(6):
-            table = cbc if e < 3 else bcf
-            both = table[e % 3, :, place]
-            turn = pltpu.roll(both, HALF // 2, 1)
-            low = lane1 < HALF // 2
-            pk[qq * 2, 4, e : e + 1, :] = jnp.where(low, both[0:1], turn[1:2])
-            pk[qq * 2 + 1, 4, e : e + 1, :] = jnp.where(low, turn[0:1], both[1:2])
+
+    def fill(p, _):
+        pk[p] = model[p % 2]
         return 0
 
-    lax.fori_loop(0, CHIPS, fill, 0)
+    lax.fori_loop(0, PLANE, fill, 0)
     stacks = [stack4(cx[e]) for e in range(3)]
     stacks += [stack4(xin[e].astype(jnp.float32)) for e in range(3)]
+    extra_rows = jnp.concatenate([extra[0:2, :]] * 4, axis=0)
+    quarter = pl.ds(pl.multiple_of(m * 512, 512), 512)
+    stacks_bc = [stack4((cbc if e < 3 else bcf)[e % 3, :, quarter]) for e in range(6)]
+    for r in range(8):
+        row = jnp.zeros((8, HALF), jnp.float32)
+        for e in range(6):
+            moved = pltpu.roll(stacks_bc[e], (FEW * (e - r)) % HALF, 1)
+            row = jnp.where(lane8 // FEW == e, moved, row)
+        for a in range(4):
+            for j in range(2):
+                pk[8 * a + r, 2 * j, 7:8, :] = row[2 * a + j : 2 * a + j + 1]
     for b in range(4):
         for h in range(2):
             row = jnp.zeros((8, HALF), jnp.float32)
             for e in range(4 * h, min(6, 4 * h + 4)):
                 moved = pltpu.roll(stacks[e], (CHUNK * (e % 4 - b)) % HALF, 1)
                 row = jnp.where(lane8 // CHUNK == e % 4, moved, row)
+            if h:
+                row = row + extra_rows
             for a in range(4):
                 for j in range(2):
                     for cc in range(2):
@@ -253,16 +255,9 @@
             axis=1,
         )
 
-    def entry_all(e):
-        both = buf[4, pl.ds(e, PLANE, stride=8), :]
-        return jnp.concatenate([both[:, : HALF // 2], both[:, HALF // 2 :]], axis=0)
-
     packed = entry(6)
-    marks = jnp.concatenate(
-        [buf[j * 2, pl.ds(7, PLANE, stride=8), :] for j in range(2)], axis=0
-    )
     turned = jnp.transpose(packed)
-    marks = jnp.transpose(marks)[0:CHUNK]
+    marks = turned[192:224]
     first = dot_nt(turned[0:96], place0)
     fresh_x = []
     fresh_marks = []
@@ -320,7 +315,10 @@
         ],
         axis=1,
     )
-    window_all = [dot_nn(place0, entry_all(e)) for e in range(3)]
+    few = jnp.concatenate(
+        [buf[2 * j, pl.ds(7, PLANE, stride=8), :] for j in range(2)], axis=0
+    )
+    window_all = dot_nn(place0, few)[:, 0 : 3 * FEW]
     for t in range(STEPS):
         new = entry(3 + t)
         if t < 2:
@@ -340,15 +338,12 @@
                 jnp.where(on, window_bc[2], window_bc[1]),
                 jnp.where(on, new, window_bc[2]),
             ]
-        new = entry_all(3 + t)
-        if t < 2:
-            new = dot_nn(places[t], new)
-        on = jnp.broadcast_to(live_cols[t], (ROWS, HALF // 2)) > 0.5
-        window_all = [
-            jnp.where(on, window_all[1], window_all[0]),
-            jnp.where(on, window_all[2], window_all[1]),
-            jnp.where(on, new, window_all[2]),
-        ]
+        new = few if t == 2 else dot_nn(places[t], few)
+        new = new[:, FEW * (3 + t) : FEW * (4 + t)]
+        on = jnp.broadcast_to(live_cols[t], (ROWS, 3 * FEW)) > 0.5
+        window_all = jnp.where(
+            on, jnp.concatenate([window_all[:, FEW:], new], axis=1), window_all
+        )
 
     def final_copy(p, part, source):
         return pltpu.make_async_remote_copy(
@@ -368,20 +363,32 @@
     to_scalar.wait()
     reads = []
 
+    wide_lane = lax.broadcasted_iota(jnp.int32, (CHUNK, HALF), 1)
+
+    def push(i, _):
+        for k in range(4):
+            f = i * 4 + k
+            for t in range(STEPS):
+                dx = jnp.where(wide_lane == f, dxs[t], 0.0)
+                dx = jnp.sum(dx, axis=1, keepdims=True)
+                dec = jnp.where(lane8 == f, decs[t], 0.0)
+                dec = jnp.sum(dec, axis=1, keepdims=True)
+                pushes[f, t] = dx * mixed[t, 0, pl.ds(f, 1), :]
+                fades[f, t] = jnp.broadcast_to(dec, (8, HALF))
+        return 0
+
+    lax.fori_loop(0, ROWS // 4, push, 0)
+
     def advance_part(part):
         def advance(j, dd, ys):
             f = j * PLANE + dd
             state = sbufs[part][sidx_s[0, f], sidx_s[1, f]].reshape(PART // 8, 8, HALF)
             here = lane == f
-            here8 = lane8 == f
             out = []
             for t in range(STEPS):
-                dx_all = dxs[t, part * PART : (part + 1) * PART, :]
-                dx = jnp.sum(jnp.where(here, dx_all, 0.0), axis=1, keepdims=True)
-                dec = jnp.sum(jnp.where(here8, decs[t], 0.0), axis=1, keepdims=True)
-                b_row = mixed[t, 0, pl.ds(f, 1), :]
                 c_row = mixed[t, 1, pl.ds(f, 1), :]
-                state = state * dec[None] + (dx * b_row).reshape(PART // 8, 8, HALF)
+                added = pushes[f, t, part * PART : (part + 1) * PART, :]
+                state = state * fades[f, t][None] + added.reshape(PART // 8, 8, HALF)
                 read = jnp.sum(state.reshape(PART, HALF) * c_row, axis=1, keepdims=True)
                 out.append(jnp.where(here, read, ys[t]))
             obuf[part, j, dd] = state.reshape(PART, HALF)
@@ -416,13 +423,12 @@
     for n in range(6):
         lo = CHUNK * (n % 4)
         flat[n // 4, :, lo : lo + CHUNK] = pieces[n]
-    for n in range(3):
-        lo = (HALF // 2) * ((n + 1) % 2)
-        flat[1 + (n + 1) // 2, :, lo : lo + HALF // 2] = window_all[n]
+    flat[1, :, 64 : 64 + 3 * FEW] = window_all
+    flat[1, :, 64 + 3 * FEW :] = jnp.zeros((ROWS, 64 - 3 * FEW), jnp.float32)
 
     def spread_rows(dd, _):
         for j in range(2):
-            for n in range(3):
+            for n in range(2):
                 ysend[dd, j : j + 1, HALF * n : HALF * (n + 1)] = flat[
                     n, pl.ds(j * PLANE + dd, 1), :
                 ]
@@ -467,6 +473,16 @@
             tile = summed if e < 3 else tiles[e // 4]
             moved = pltpu.roll(tile, (CHUNK * (b - e % 4)) % HALF, 1)
             wide[e] = jnp.where(lane8 // CHUNK == b, moved, wide[e])
+    closing = [jnp.zeros((8, HALF), jnp.float32)] * 3
+    for r in range(8):
+        tile = jnp.concatenate(
+            [yrecv[8 * a + r, :, HALF : 2 * HALF] for a in range(4)], axis=0
+        )
+        for e in range(3):
+            moved = pltpu.roll(tile, (FEW * (r - e) - 64) % HALF, 1)
+            closing[e] = jnp.where(lane8 // FEW == r, moved, closing[e])
+    for e in range(3):
+        ends[m, e] = closing[e]
     gated = []
     squares = jnp.zeros((8, HALF), jnp.float32)
     for t in range(STEPS):
@@ -483,22 +499,23 @@
         )
         copy.start()
         sq_copies.append(copy)
-    low = lane8[0:2] < HALF // 2
+        copy = pltpu.make_async_remote_copy(
+            src_ref=ends.at[m], dst_ref=ends.at[m],
+            send_sem=q_ss.at[3 + n], recv_sem=q_rs.at[3 + n],
+            device_id=peer, device_id_type=MESH,
+        )
+        copy.start()
+        sq_copies.append(copy)
     for a in range(4):
         for e in range(3):
             out_x[e, :, HALF * a : HALF * (a + 1)] = wide[3 + e][2 * a : 2 * a + 2]
-    for qq in range(CHIPS):
-        for e in range(3):
-            tile = HALF * (1 + (e + 1) // 2)
-            left = yrecv[2 * qq, :, tile : tile + HALF]
-            right = yrecv[2 * qq + 1, :, tile : tile + HALF]
-            if e == 1:
-                right = pltpu.roll(right, HALF // 2, 1)
-            else:
-                left = pltpu.roll(left, HALF // 2, 1)
-            out_bc[e, :, HALF * qq : HALF * (qq + 1)] = jnp.where(low, left, right)
     for copy in sq_copies:
         copy.wait()
+    for n in range(SIDE):
+        for e in range(3):
+            for a in range(4):
+                lo = 512 * n + HALF * a
+                out_bc[e, :, lo : lo + HALF] = ends[n, e, 2 * a : 2 * a + 2, :]
     total = sqsend[...] + sqrecv[0] + sqrecv[1] + sqrecv[2]
     even = lax.broadcasted_iota(jnp.int32, (8, HALF), 0) % 2 == 0
     gains = jnp.concatenate([gain[n // 2 : n // 2 + 1, :] for n in range(8)], axis=0)
@@ -587,17 +604,20 @@
             pltpu.SMEM((8,), f32),
             pltpu.SMEM((8,), f32),
             dma((16,)),
-            pltpu.VMEM((PLANE, 5, 8, HALF), f32),
-            pltpu.VMEM((5, PLANE * 8, HALF), f32),
+            pltpu.VMEM((PLANE, 4, 8, HALF), f32),
+            pltpu.VMEM((4, PLANE * 8, HALF), f32),
             pltpu.VMEM((2, PLANE, PART, HALF), f32),
             pltpu.VMEM((2, PLANE, PART, HALF), f32),
             pltpu.VMEM((PARTS, 2, PLANE, PART, HALF), f32),
             pltpu.VMEM((STEPS, CHUNK, HALF), f32),
             pltpu.VMEM((STEPS, 8, HALF), f32),
             pltpu.VMEM((STEPS, 2, ROWS, HALF), f32),
-            pltpu.VMEM((3, ROWS, HALF), f32),
-            pltpu.VMEM((PLANE, 2, 384), f32),
-            pltpu.VMEM((PLANE, 2, 384), f32),
+            pltpu.VMEM((2, ROWS, HALF), f32),
+            pltpu.VMEM((PLANE, 2, 256), f32),
+            pltpu.VMEM((PLANE, 2, 256), f32),
+            pltpu.VMEM((SIDE, 3, 8, HALF), f32),
+            pltpu.VMEM((ROWS, STEPS, CHUNK, HALF), f32),
+            pltpu.VMEM((ROWS, STEPS, 8, HALF), f32),
             pltpu.VMEM((8, HALF), f32),
             pltpu.VMEM((3, 8, HALF), f32),
             pltpu.VMEM((8, HALF), jnp.int32),
@@ -609,7 +629,7 @@
             dma((PARTS, PLANE)), dma((PARTS, PLANE)),
             dma((PARTS, PLANE)), dma((PARTS, PLANE)),
             dma((PLANE,)), dma((PLANE,)),
-            dma((4,)), dma((4,)),
+            dma((8,)), dma((8,)),
             dma((8,)),
         ],
         compiler_params=pltpu.CompilerParams(

time: 52.5 us -> 49.7 us (0.947)
  Pallas kernels: 51.6 us -> 48.8 us
    pallas_call x1, Pallas kernels: 49.3 us -> 46.6 us  [local(): pl.pallas_call(kernel, out_shape=tuple(shapes), in_specs=[hbm] * (1 + FIX...]
where the time goes in v4:
time: 49.7 us; the launch traced here: 49.5 us
  Pallas kernels  48.8 us (98%)
  between operations  0.65 us (1%)
    pallas_call x1, Pallas kernels, local(): pl.pallas_call(kernel, out_shape=tuple(shapes), in_specs=[hbm] * (1 + FIX...  46.6 us
    pallas_call x1, Pallas kernels, local(): pl.pallas_call(finish, out_shape=(shapes[0], shapes[2], shapes[3], bits),...  2.27 us

profile of v4, /device:TPU:1, one launch (start us, length us, event | category | flops | bytes accessed | tf_op | source)
XLA Modules:
  0.0 49.5 jit_solution(17788337952485282964)
XLA Ops:
  0.6 46.6 %shard_map.183 = (f32[2,512,256]{2,1,0:T(8,128)}, f32[3,2,512]{2,1,0:T(2,128)}, f32[3,2,512]{2,1,0:T(2,128)}, f32[3,2,2048]{2,1,0:T(2,128)}) custom-call(f32[2,512,256]{2,1,0:T(8,128)} %bitcast.8, f32[3,2,512]{2,1,0:T(2,128)} %bitcast.10, bf16[3,2,512]{2,1,0:T(2,128)(2,1)} %refs_1_.1, f32[3,2,2048]{2,1,0:T(2,128)} %bitcast.9, bf16[3,2,2048]{2,1,0:T(2,128)(2,1)} %refs_3_.1, ...), custom_call_target="tpu_custom_call" | custom-call | tf_op jit(solution)/shard_map/pallas_call | solution.py:585
  47.2 2.3 %shard_map.184 = (f32[2,512,256]{2,1,0:T(8,128)}, f32[3,2,512]{2,1,0:T(2,128)}, f32[3,2,2048]{2,1,0:T(2,128)}, bf16[3,2,512]{2,1,0:T(2,128)(2,1)}) custom-call(f32[2,512,256]{2,1,0:T(8,128)} %get-tuple-element.12.refs_0_, f32[3,2,512]{2,1,0:T(2,128)} %get-tuple-element.13.refs_1_, f32[3,2,2048]{2,1,0:T(2,128)} %get-tuple-element.14.refs_2_, ...), custom_call_target="tpu_custom_call" | custom-call | tf_op jit(solution)/shard_map/pallas_call | solution.py:645

commit v5 on v4

--- a/solution.py
+++ b/solution.py
@@ -96,8 +96,6 @@
         pltpu.make_async_copy(source, target, in_sem.at[n])
         for n, (source, target) in enumerate(zip(given, held))
     ]
-    for copy in loads:
-        copy.start()
     barrier = pltpu.get_barrier_semaphore()
     signals = 0
     for offset in OFFSETS:
@@ -106,6 +104,9 @@
     for peer in norm_peers:
         pl.semaphore_signal(barrier, inc=1, device_id=peer, device_id_type=MESH)
         signals += 1
+
+    for copy in loads:
+        copy.start()
 
     for copy in loads:
         copy.wait()
@@ -363,6 +364,25 @@
     to_scalar.wait()
     reads = []
 
+    backs = [eye if t == 2 else dot_nt(eye, places[t]) for t in range(STEPS)]
+    for t in range(STEPS):
+        lo = CHUNK * ((3 + t) % 4)
+        flat[(3 + t) // 4, :, lo : lo + CHUNK] = dot_nt(eye, window[t])
+    flat[1, :, 64 : 64 + 3 * FEW] = window_all
+    flat[1, :, 64 + 3 * FEW :] = jnp.zeros((ROWS, 64 - 3 * FEW), jnp.float32)
+
+    def spread_rows(n):
+        def spread(dd, _):
+            for j in range(2):
+                ysend[dd, j : j + 1, HALF * n : HALF * (n + 1)] = flat[
+                    n, pl.ds(j * PLANE + dd, 1), :
+                ]
+            return 0
+
+        lax.fori_loop(0, PLANE, spread, 0)
+
+    spread_rows(1)
+
     wide_lane = lax.broadcasted_iota(jnp.int32, (CHUNK, HALF), 1)
 
     def push(i, _):
@@ -413,28 +433,10 @@
                 final_copy(at(offset)[0], part, d).start()
             own_finals[part].start()
 
-    pieces = [None] * 6
     for t in range(STEPS):
         read = jnp.concatenate([part[t][:, 0:ROWS] for part in reads], axis=0)
-        read = read + skipped[t]
-        back = eye if t == 2 else dot_nt(eye, places[t])
-        pieces[t] = dot_nt(back, read)
-        pieces[3 + t] = dot_nt(eye, window[t])
-    for n in range(6):
-        lo = CHUNK * (n % 4)
-        flat[n // 4, :, lo : lo + CHUNK] = pieces[n]
-    flat[1, :, 64 : 64 + 3 * FEW] = window_all
-    flat[1, :, 64 + 3 * FEW :] = jnp.zeros((ROWS, 64 - 3 * FEW), jnp.float32)
-
-    def spread_rows(dd, _):
-        for j in range(2):
-            for n in range(2):
-                ysend[dd, j : j + 1, HALF * n : HALF * (n + 1)] = flat[
-                    n, pl.ds(j * PLANE + dd, 1), :
-                ]
-        return 0
-
-    lax.fori_loop(0, PLANE, spread_rows, 0)
+        flat[0, :, CHUNK * t : CHUNK * (t + 1)] = dot_nt(backs[t], read + skipped[t])
+    spread_rows(0)
 
     def read_copy(p, source):
         return pltpu.make_async_remote_copy(
@@ -546,6 +548,10 @@
 
 def finish(*refs):
     given, outs, held, mixer, sems = refs[:4], refs[4:8], refs[8:12], refs[12], refs[13]
+    def ends(refs):
+        return (refs[0].at[0], refs[0].at[1], *refs[1:])
+
+    given, held, outs = ends(given), ends(held), ends(outs)
     loads = [
         pltpu.make_async_copy(source, target, sems.at[0, n])
         for n, (source, target) in enumerate(zip(given, held))
@@ -554,16 +560,14 @@
         copy.start()
     stores = [
         pltpu.make_async_copy(source, target, sems.at[1, n])
-        for n, (source, target) in enumerate(zip((*held[:3], mixer), outs))
+        for n, (source, target) in enumerate(zip((*held[:4], mixer), outs))
     ]
-    for n in (1, 2):
+    for n in (0, 1, 2, 3):
         loads[n].wait()
         stores[n].start()
-    loads[3].wait()
-    mixer[...] = held[3][...].astype(jnp.bfloat16)
-    stores[3].start()
-    loads[0].wait()
-    stores[0].start()
+    loads[4].wait()
+    mixer[...] = held[4][...].astype(jnp.bfloat16)
+    stores[4].start()
     for copy in stores:
         copy.wait()
 
@@ -649,7 +653,7 @@
         out_specs=(hbm,) * 4,
         scratch_shapes=[
             pltpu.VMEM(shapes[n].shape, f32) for n in (0, 2, 3, 1)
-        ] + [pltpu.VMEM(bits.shape, jnp.bfloat16), dma((2, 4))],
+        ] + [pltpu.VMEM(bits.shape, jnp.bfloat16), dma((2, 5))],
         compiler_params=pltpu.CompilerParams(vmem_limit_bytes=VMEM_BYTES),
     )(state, final_x, final_bc, mix)
     return (

time: 49.7 us -> 49.4 us (level)
  no operation moved by 1% of the time
where the time goes in v5:
time: 49.4 us; the launch traced here: 49.2 us
  Pallas kernels  48.6 us (98%)
  between operations  0.65 us (1%)
    pallas_call x1, Pallas kernels, local(): pl.pallas_call(kernel, out_shape=tuple(shapes), in_specs=[hbm] * (1 + FIX...  46.5 us
    pallas_call x1, Pallas kernels, local(): pl.pallas_call(finish, out_shape=(shapes[0], shapes[2], shapes[3], bits),...  2.1 us

profile of v5, /device:TPU:1, one launch (start us, length us, event | category | flops | bytes accessed | tf_op | source)
XLA Modules:
  0.0 49.2 jit_solution(1197441008911024924)
XLA Ops:
  0.6 46.5 %shard_map.183 = (f32[2,512,256]{2,1,0:T(8,128)}, f32[3,2,512]{2,1,0:T(2,128)}, f32[3,2,512]{2,1,0:T(2,128)}, f32[3,2,2048]{2,1,0:T(2,128)}) custom-call(f32[2,512,256]{2,1,0:T(8,128)} %bitcast.8, f32[3,2,512]{2,1,0:T(2,128)} %bitcast.10, bf16[3,2,512]{2,1,0:T(2,128)(2,1)} %refs_1_.1, f32[3,2,2048]{2,1,0:T(2,128)} %bitcast.9, bf16[3,2,2048]{2,1,0:T(2,128)(2,1)} %refs_3_.1, ...), custom_call_target="tpu_custom_call" | custom-call | tf_op jit(solution)/shard_map/pallas_call | solution.py:589
  47.1 2.1 %shard_map.184 = (f32[2,512,256]{2,1,0:T(8,128)}, f32[3,2,512]{2,1,0:T(2,128)}, f32[3,2,2048]{2,1,0:T(2,128)}, bf16[3,2,512]{2,1,0:T(2,128)(2,1)}) custom-call(f32[2,512,256]{2,1,0:T(8,128)} %get-tuple-element.12.refs_0_, f32[3,2,512]{2,1,0:T(2,128)} %get-tuple-element.13.refs_1_, f32[3,2,2048]{2,1,0:T(2,128)} %get-tuple-element.14.refs_2_, ...), custom_call_target="tpu_custom_call" | custom-call | tf_op jit(solution)/shard_map/pallas_call | solution.py:649
